TPU v7x, 256 devices: a whole 4x4x8 slice. The times are simulated.
256 devices in a mesh: stretch: 64 (over x, z_lo, y), head: 4 (over z_hi, core).
Axes of the slice: x: 4, y: 4, z: 8 (z_hi: 2, z_lo: 4; z = z_hi * 4 + z_lo), core: 2. Of those that a mesh axis runs over, the one named last changes fastest.
Arguments:
- queries: bfloat16 [8192, 6144], P('stretch', 'head'), may hold values from -92 to 92
- keys: bfloat16 [8192, 1024], P('stretch', 'head'), may hold values from -11 to 11
- values: bfloat16 [8192, 1024], P('stretch', 'head'), may hold values from -6 to 6
- cache_keys: bfloat16 [4096, 1024], P(('stretch', 'head')), may hold values from -100 to 100
- cache_values: bfloat16 [4096, 1024], P(('stretch', 'head')), may hold values from -6 to 6
- page_owner: int32 [64], replicated, may hold values from 0 to 63, each once
- window: int32 [4], replicated, may hold values from 1 to 2, as said below
Outputs:
- attended: bfloat16 [8192, 6144], P('stretch', 'head')
Inputs may be any that keep to these rules, and one draw needn't show every extreme that they name: `window`: some in-flight stretch attends all 2 cached stretches.
All inputs are finite; a program needn't handle non-finite values.
Results may differ from a plain program's by a relative error of at most 0.006.
Values may be sent and summed in bfloat16 or wider, within the bound.
No kernel may reach another device: no remote copies, remote signals or barrier semaphores. Data moves between devices by JAX's collectives and lax.ppermute only.
A program may use at most 192 MiB of HBM per device.

v0:
```python
import jax
import jax.numpy as jnp
from jax import lax
from jax.experimental import pallas as pl
from jax.experimental.pallas import tpu as pltpu
from jax.sharding import Mesh, PartitionSpec as P

D = 128
GROUP = 6
WIDE = GROUP * D
HALF = 64
CROWS = 32
BLOCK = HALF + CROWS
MESSAGE = BLOCK + 3 * HALF
ROWS = GROUP * HALF
NEG = -1e30
SCALE = D**-0.5 * 1.4426950408889634

VMEM = pltpu.VMEM
BF = jnp.bfloat16
F32 = jnp.float32
vmem = pl.BlockSpec(memory_space=VMEM)
smem = pl.BlockSpec(memory_space=pltpu.SMEM)


def shaped(shape, dtype=BF):
    return jax.ShapeDtypeStruct(shape, dtype)


def slot():
    return 2 * (lax.axis_index("x") & 1) + lax.axis_index("core")


def aligned(index, step):
    return pl.ds(pl.multiple_of(index * step, step), step)


def deal_body(q_ref, k_ref, v_ref, ck_ref, cv_ref, q_got, k_got, v_got, c_got, *outs):
    x, half, core = lax.axis_index("x"), lax.axis_index("zh"), lax.axis_index("core")
    rows = aligned(core, HALF)
    for s in range(4):
        head = (x + s) & 3
        out = outs[s]

        def from_core(q, k, v, out=out, e=head & 1):
            out[:HALF, :D] = k[rows, aligned(e, D)]
            out[:HALF, D:] = v[rows, aligned(e, D)]
            for i in range(3):
                lanes = pl.ds(pl.multiple_of(e * WIDE + i * 2 * D, D), 2 * D)
                out[BLOCK + i * HALF : BLOCK + (i + 1) * HALF, :] = q[rows, lanes]

        @pl.when((head >> 1) == core)
        def _():
            from_core(q_ref, k_ref, v_ref)

        @pl.when((head >> 1) != core)
        def _():
            from_core(q_got, k_got, v_got)

        lanes = aligned(half * 4 + head, D)
        out[HALF : HALF + 16, :D] = ck_ref[:, lanes]
        out[HALF : HALF + 16, D:] = cv_ref[:, lanes]
        lanes = aligned(head, D)
        out[HALF + 16 : BLOCK, :D] = c_got[:16, lanes]
        out[HALF + 16 : BLOCK, D:] = c_got[16:, lanes]


def deal(own, got):
    return pl.pallas_call(
        deal_body, out_shape=[shaped((MESSAGE, 2 * D))] * 4, name="deal"
    )(*own, *got)


def join_body(*refs):
    x = lax.axis_index("x")
    block, q = refs[4:]
    for s in range(4):
        source = pl.ds((x + 4 - s) & 3, 1)
        block[source] = refs[s][:BLOCK, :][None]
        q[source] = refs[s][BLOCK:, :][None]


def join(messages):
    return pl.pallas_call(
        join_body,
        out_shape=[shaped((4, BLOCK, 2 * D)), shaped((4, 3 * HALF, 2 * D))],
        name="join",
    )(*messages)


def attend_body(first, last, refs):
    window_ref, bias_ref, *refs = refs
    q_refs, refs = refs[:2], refs[2:]
    if not first:
        acc, top, *refs = refs
    q_all, keys, vals, *made = refs[-4:] if last else refs[-3:]
    blocks, outs = (refs[:-8], refs[-8:-4]) if last else (refs[:-5], refs[-5:-3])
    blocks = [pair.at[i] for pair in blocks for i in range(2)]
    total = keys.shape[0]
    for h in range(2):
        for c in range(4):
            for g in range(GROUP):
                rows = slice(g // 2 * HALF, (g // 2 + 1) * HALF)
                part = q_refs[h][c, rows, g % 2 * D : (g % 2 + 1) * D]
                q_all[h, c, g * HALF : (g + 1) * HALF, :] = part
    at = 0
    for t in range(-4, 4):
        for block in blocks:
            part = block[t + 4, HALF:, :] if t < 0 else block[t, :HALF, :]
            depth = part.shape[0]
            keys[at : at + depth, :] = part[:, :D]
            vals[at : at + depth, :D] = part[:, D:]
            at += depth
    vals[:, D:] = jnp.ones((total, D), BF)
    paged = 4 * CROWS * len(blocks)
    core = lax.axis_index("core")
    lane = lax.broadcasted_iota(jnp.int32, (HALF, D), 1)

    def seen(c):
        return paged + (c + 1) * HALF * len(blocks)

    def scores(h, c):
        s = lax.dot_general(
            q_all[h, c], keys[: seen(c), :], (((1,), (1,)), ((), ())), preferred_element_type=F32
        )
        bias = jnp.where(window_ref[c] > 1, 0.0, bias_ref[...])
        return jnp.concatenate([s[:, :paged] + bias, s[:, paged:]], axis=1)

    def absorb(h, c, s):
        new = jnp.max(s, axis=1, keepdims=True)
        if first:
            new = jnp.broadcast_to(new, (ROWS, D))
        else:
            old = top[h, c]
            new = jnp.maximum(old, new)
        p = jnp.exp2((s - new[:, :1]) * SCALE).astype(BF)
        update = jnp.dot(p, vals[: seen(c), :], preferred_element_type=F32)
        out, norm = update[:, :D], update[:, D:]
        if not first:
            factor = jnp.exp2((old - new) * SCALE)
            out, norm = acc[h, c, :, :D] * factor + out, acc[h, c, :, D:] * factor + norm
        if not last:
            outs[0][h, c, :, :D] = out
            outs[0][h, c, :, D:] = norm
            outs[1][h, c] = new
            return
        out = (out / norm).astype(BF)
        log = new * SCALE + jnp.log2(norm)
        rows = aligned((core + h) & 1, HALF)
        logs = jnp.zeros((HALF, D), F32)
        for g in range(GROUP):
            part = slice(g * HALF, (g + 1) * HALF)
            made[0][c, rows, g * D : (g + 1) * D] = out[part, :]
            left = log[part, :]
            for i in range(3):
                term = left.astype(BF).astype(F32)
                logs = jnp.where(lane == 3 * g + i, term, logs)
                left = left - term
        made[0][c, rows, WIDE:] = logs.astype(BF)

    def token_half(h, carry):
        ahead = scores(h, 3)
        for c in (3, 2, 1, 0):
            now, ahead = ahead, scores(h, c - 1) if c else None
            absorb(h, c, now)
        return carry

    lax.fori_loop(0, 2, token_half, 0)
    if last:
        r = slot()
        for s in range(4):
            outs[s][...] = made[0][r ^ s]


def attend(q, state, pairs, window, bias, last=False):
    total = BLOCK * 8 * len(pairs)
    kept = [] if state is None else list(state)
    work = 16 * ROWS * len(pairs) * (4 * CROWS + 2.5 * HALF)
    if last:
        shapes = [shaped((2 * HALF, WIDE + D))] * 4
    else:
        shapes = [shaped((2, 4, ROWS, 2 * D), F32), shaped((2, 4, ROWS, D), F32)]
    return pl.pallas_call(
        lambda *refs: attend_body(state is None, last, refs),
        in_specs=[smem] + [vmem] * (3 + len(kept) + len(pairs)),
        out_specs=[vmem] * len(shapes),
        out_shape=shapes,
        scratch_shapes=[
            VMEM((2, 4, ROWS, D), BF),
            VMEM((total, D), BF),
            VMEM((total, 2 * D), BF),
        ]
        + ([VMEM((4, 2 * HALF, WIDE + D), BF)] if last else []),
        compiler_params=pltpu.CompilerParams(vmem_limit_bytes=40 * 2**20),
        cost_estimate=pl.CostEstimate(
            flops=int(work * D * 4 * 2), bytes_accessed=2**20, transcendentals=int(work)
        ),
        name="attend",
    )(window, bias, *q, *kept, *pairs)


def merge_body(*refs):
    out = refs[4]
    x = lax.axis_index("x")
    lane = lax.broadcasted_iota(jnp.int32, (D, WIDE), 0)
    head = lax.broadcasted_iota(jnp.int32, (D, WIDE), 1) // D
    pick = jnp.where((lane // 3 == head) & (lane < 3 * GROUP), 1.0, 0.0).astype(BF)
    for pair in range(2):
        one, two = refs[2 * pair], refs[2 * pair + 1]
        a, b = (jnp.dot(ref[:, WIDE:], pick, preferred_element_type=F32) for ref in (one, two))
        most = jnp.maximum(a, b)
        a, b = jnp.exp2(a - most), jnp.exp2(b - most)
        both = (one[:, :WIDE].astype(F32) * a + two[:, :WIDE].astype(F32) * b) / (a + b)
        out[:, aligned((x >> 1) ^ pair, WIDE)] = both.astype(BF)


def merge(messages):
    return pl.pallas_call(
        merge_body, out_shape=shaped((2 * HALF, 2 * WIDE)), name="merge"
    )(*messages)


def spread(s):
    pairs = []
    for x in range(4):
        for core in range(2):
            piece = x ^ s
            pairs.append((x * 2 + core, (2 * core + (piece >> 1)) * 2 + (piece & 1)))
    return pairs


def shift(array, axis, by, size=4):
    return lax.ppermute(array, axis, [(i, (i + by) % size) for i in range(size)])


def swap(array):
    return shift(array, "core", 1, 2)


RING = (0, 2, 3, 1)


def loop_pairs(axis_of_core, by):
    pairs = []
    for zl in range(4):
        for y in range(4):
            for core in range(2):
                z2, y2 = zl, y
                if axis_of_core[core] == "y":
                    y2 = (y + by) % 4
                else:
                    z2 = RING[(RING.index(zl) + by) % 4]
                pairs.append(((zl * 4 + y) * 2 + core, (z2 * 4 + y2) * 2 + core))
    return pairs


def step_on(block, phase, by=1):
    pairs = loop_pairs(("zl", "y") if phase == 0 else ("y", "zl"), by)
    return lax.ppermute(block, ("zl", "y", "core"), pairs)


def cache_bias(page_owner, blocks):
    zl, y, core = lax.axis_index("zl"), lax.axis_index("y"), lax.axis_index("core")
    shape = (4, len(blocks), CROWS)
    xs = lax.broadcasted_iota(jnp.int32, shape, 0)
    n = lax.broadcasted_iota(jnp.int32, shape, 1)
    a = b = jnp.zeros(shape, jnp.int32)
    for i, (a_steps, b_steps) in enumerate(blocks):
        a, b = jnp.where(n == i, a_steps, a), jnp.where(n == i, b_steps, b)
    z_steps, y_steps = jnp.where(core == 0, a, b), jnp.where(core == 0, b, a)
    index = jnp.where(zl == 0, 0, jnp.where(zl == 2, 1, jnp.where(zl == 3, 2, 3)))
    at = (index + 4 - z_steps) & 3
    zs = jnp.where(at == 0, 0, jnp.where(at == 1, 2, jnp.where(at == 2, 3, 1)))
    page = (xs * 4 + zs) * 4 + ((y + 4 - y_steps) & 3)
    page = page.reshape(1, -1, 1)
    late = jnp.any(page == page_owner[None, None, 32:], axis=2)
    return jnp.where(late, 0.0, NEG).astype(F32)


PAIRS = ((0, 1), (3, 2))
PIECES = (
    ((0, 0),),
    ((1, 0), (0, 1)),
    ((1, 1), (0, 2)),
    ((1, 2), (0, 3)),
    ((1, 3),),
)
MOVES = (
    ((0, 1),),
    ((1, 1), (0, 2)),
    ((1, 2), (0, 3)),
    ((1, 3),),
    (),
)


def on_device(queries, keys, values, cache_keys, cache_values, page_owner, window):
    got = [swap(one) for one in (queries, keys, values)]
    start = 4 * D * (1 - lax.axis_index("zh"))
    halves = [lax.dynamic_slice_in_dim(c, start, 4 * D, 1) for c in (cache_keys, cache_values)]
    got.append(shift(jnp.concatenate(halves), "zh", 1, 2))
    messages = deal((queries, keys, values, cache_keys, cache_values), got)
    messages = [messages[0]] + [shift(messages[s], "x", s) for s in range(1, 4)]
    block, mine = join(messages)
    q = [mine, swap(mine)]
    first = step_on(block, 0)
    third = step_on(block, 0, 3)
    second = step_on(first, 0)
    pairs = {(0, 0): jnp.stack([block, first])}
    state = None
    for piece, moves in zip(PIECES, MOVES):
        if state is not None and (1, 0) not in pairs:
            third, second, *state = lax.optimization_barrier((third, second, *state))
            pairs[1, 0] = jnp.stack([third, second])
        for pair, b in moves:
            before = pairs[pair, b - 1]
            if state is not None:
                before, *state = lax.optimization_barrier((before, *state))
            pairs[pair, b] = step_on(before, 1)
        state = attend(
            q,
            state,
            [pairs[one] for one in piece],
            window,
            cache_bias(page_owner, [(a, b) for pair, b in piece for a in PAIRS[pair]]),
            last=piece is PIECES[-1],
        )
    back = [
        lax.ppermute(state[s], ("x", "core"), [(b, a) for a, b in spread(s)]) for s in range(4)
    ]
    return merge(back)


def solution(mesh):
    fine = Mesh(mesh.devices.reshape(4, 4, 4, 2, 2), ("x", "zl", "y", "zh", "core"))
    tokens, heads = ("x", "zl", "y"), ("zh", "core")
    return jax.shard_map(
        on_device,
        mesh=fine,
        in_specs=(
            P(tokens, heads),
            P(tokens, heads),
            P(tokens, heads),
            P(tokens + heads, None),
            P(tokens + heads, None),
            P(),
            P(),
        ),
        out_specs=P(tokens, heads),
        check_vma=False,
    )
```

profile of v0, /device:TPU:1, one launch (start us, length us, event | category | flops | bytes accessed | tf_op | source)
XLA Modules:
  0.0 99.1 jit_solution(6160037133305725653)
XLA Ops:
  0.0 0.7 constant_dynamic-slice_fusion
  0.7 7.7 %collective-permute-start.3 = (bf16[32,512]{1,0:T(8,128)(2,1)S(1)}, bf16[32,512]{1,0:T(8,128)(2,1)S(1)}, u32[]{:S(2)}, u32[]{:S(2)}) collective-permute-start(bf16[32,512]{1,0:T(8,128)(2,1)S(1)} %pad_maximum_fusion.2), channel_id=1, source_target_pairs={{0,2},{2,0},{1,3},{3,1},{4,6},{6,4},{5,7},{7,5},{8,10},{10,8},{9,1... | collective-permute-start | bytes 98312 | tf_op jit(solution)/shard_map/ppermute | solution.py:233
  8.5 1.0 collective-permute-start
  9.4 0.5 collective-permute-start.2
  10.2 0.7 slice.2
  11.2 0.1 compare_reduce_fusion
  11.5 0.6 copy-done.12
  12.2 0.7 copy-done.2
  12.9 2.1 %deal.1 = (bf16[288,256]{1,0:T(8,128)(2,1)}, bf16[288,256]{1,0:T(8,128)(2,1)}, bf16[288,256]{1,0:T(8,128)(2,1)}, bf16[288,256]{1,0:T(8,128)(2,1)}) custom-call(bf16[128,1536]{1,0:T(8,128)(2,1)} %q_ref.1, bf16[128,256]{1,0:T(8,128)(2,1)} %k_ref.1, bf16[128,256]{1,0:T(8,128)(2,1)} %v_ref.1, bf16[16,1024]{1,0:T(8,128)(2,1)} %ck_ref.1, bf16[16,1024]{1,0:T(8,128)(2,1)} %cv_ref.1, ...), custom_call_target="tpu_custom_call" | custom-call | tf_op jit(solution)/shard_map/deal/pallas_call | solution.py:69
  15.0 1.2 %collective-permute-start.4 = (bf16[288,256]{1,0:T(8,128)(2,1)}, bf16[288,256]{1,0:T(8,128)(2,1)S(1)}, u32[]{:S(2)}, u32[]{:S(2)}) collective-permute-start(bf16[288,256]{1,0:T(8,128)(2,1)} %get-tuple-element.43), channel_id=1, source_target_pairs={{0,64},{64,128},{128,192},{192,0},{1,65},{65,129},{129,193},{193,1... | collective-permute-start | bytes 442376 | tf_op jit(solution)/shard_map/ppermute | solution.py:233
  16.3 2.5 %collective-permute-start.5 = (bf16[288,256]{1,0:T(8,128)(2,1)}, bf16[288,256]{1,0:T(8,128)(2,1)S(1)}, u32[]{:S(2)}, u32[]{:S(2)}) collective-permute-start(bf16[288,256]{1,0:T(8,128)(2,1)} %get-tuple-element.44), channel_id=1, source_target_pairs={{0,128},{64,192},{128,0},{192,64},{1,129},{65,193},{129,1},{193,65... | collective-permute-start | bytes 442376 | tf_op jit(solution)/shard_map/ppermute | solution.py:233
  18.7 1.2 %collective-permute-start.6 = (bf16[288,256]{1,0:T(8,128)(2,1)}, bf16[288,256]{1,0:T(8,128)(2,1)S(1)}, u32[]{:S(2)}, u32[]{:S(2)}) collective-permute-start(bf16[288,256]{1,0:T(8,128)(2,1)} %get-tuple-element.45), channel_id=1, source_target_pairs={{0,192},{64,0},{128,64},{192,128},{1,193},{65,1},{129,65},{193,129... | collective-permute-start | bytes 442376 | tf_op jit(solution)/shard_map/ppermute | solution.py:233
  19.9 1.7 %collective-permute-done.4.refs_1_ = bf16[288,256]{1,0:T(8,128)(2,1)S(1)} collective-permute-done((bf16[288,256]{1,0:T(8,128)(2,1)}, bf16[288,256]{1,0:T(8,128)(2,1)S(1)}, u32[]{:S(2)}, u32[]{:S(2)}) %collective-permute-start.4) | collective-permute-done | bytes 147488 | tf_op jit(solution)/shard_map/ppermute | solution.py:233
  21.6 4.5 %collective-permute-done.5.refs_2_ = bf16[288,256]{1,0:T(8,128)(2,1)S(1)} collective-permute-done((bf16[288,256]{1,0:T(8,128)(2,1)}, bf16[288,256]{1,0:T(8,128)(2,1)S(1)}, u32[]{:S(2)}, u32[]{:S(2)}) %collective-permute-start.5) | collective-permute-done | bytes 147488 | tf_op jit(solution)/shard_map/ppermute | solution.py:233
  26.1 0.7 copy-done.8
  26.8 2.0 %join.1 = (bf16[4,96,256]{2,1,0:T(8,128)(2,1)}, bf16[4,192,256]{2,1,0:T(8,128)(2,1)}) custom-call(bf16[288,256]{1,0:T(8,128)(2,1)} %get-tuple-element.42.refs_0_, bf16[288,256]{1,0:T(8,128)(2,1)} %copy-done.7, bf16[288,256]{1,0:T(8,128)(2,1)} %copy-done.8, bf16[288,256]{1,0:T(8,128)(2,1)} %copy-done.9), custom_call_target="tpu_custom_call" | custom-call | tf_op jit(solution)/shard_map/join/pallas_call | solution.py:84
  28.8 0.8 collective-permute-start.7
  29.6 0.1 compare_reduce_fusion.3
  29.7 1.4 %collective-permute-start.9 = (bf16[4,96,256]{2,1,0:T(8,128)(2,1)}, bf16[4,96,256]{2,1,0:T(8,128)(2,1)S(1)}, u32[]{:S(2)}, u32[]{:S(2)}) collective-permute-start(bf16[4,96,256]{2,1,0:T(8,128)(2,1)} %get-tuple-element.47), channel_id=1, source_target_pairs={{0,32},{1,5},{4,36},{5,9},{8,40},{9,13},{12,44},{13,1},{16,0},{17,... | collective-permute-start | bytes 589832 | tf_op jit(solution)/shard_map/ppermute | solution.py:259
  31.0 1.5 %collective-permute-start.8 = (bf16[4,96,256]{2,1,0:T(8,128)(2,1)}, bf16[4,96,256]{2,1,0:T(8,128)(2,1)S(1)}, u32[]{:S(2)}, u32[]{:S(2)}) collective-permute-start(bf16[4,96,256]{2,1,0:T(8,128)(2,1)} %get-tuple-element.47), channel_id=1, source_target_pairs={{0,16},{1,13},{4,20},{5,1},{8,24},{9,5},{12,28},{13,9},{16,48},{17... | collective-permute-start | bytes 589832 | tf_op jit(solution)/shard_map/ppermute | solution.py:259
  32.6 3.3 %collective-permute-done.9 = bf16[4,96,256]{2,1,0:T(8,128)(2,1)S(1)} collective-permute-done((bf16[4,96,256]{2,1,0:T(8,128)(2,1)}, bf16[4,96,256]{2,1,0:T(8,128)(2,1)S(1)}, u32[]{:S(2)}, u32[]{:S(2)}) %collective-permute-start.9) | collective-permute-done | bytes 196640 | tf_op jit(solution)/shard_map/ppermute | solution.py:259
  35.9 0.2 collective-permute-start.10
  36.1 1.0 pad_maximum_fusion.refs_4_
  37.0 1.3 %collective-permute-start.12 = (bf16[2,4,96,256]{3,2,1,0:T(8,128)(2,1)S(1)}, bf16[2,4,96,256]{3,2,1,0:T(8,128)(2,1)S(1)}, u32[]{:S(2)}, u32[]{:S(2)}) collective-permute-start(bf16[2,4,96,256]{3,2,1,0:T(8,128)(2,1)S(1)} %pad_maximum_fusion.refs_4_), channel_id=1, source_target_pairs={{0,4},{1,33},{4,8},{5,37},{8,12},{9,41},{12,0},{13,45},{16,20},{17... | collective-permute-start | bytes 1179656 | tf_op jit(solution)/shard_map/ppermute | solution.py:259
  38.3 1.0 %copy-done = bf16[4,192,256]{2,1,0:T(8,128)(2,1)S(1)} copy-done((bf16[4,192,256]{2,1,0:T(8,128)(2,1)S(1)}, bf16[4,192,256]{2,1,0:T(8,128)(2,1)}, u32[]{:S(2)}) %copy-start) | copy-done | bytes 393240
  39.3 0.7 copy-done.1
  40.0 3.7 %attend.5 = (f32[2,4,384,256]{3,2,1,0:T(8,128)S(1)}, f32[2,4,384,128]{3,2,1,0:T(8,128)S(1)}) custom-call(s32[4]{0:T(128)S(1)} %copy-done.1, f32[1,256]{1,0:T(1,128)S(1)} %bitcast.13, bf16[4,192,256]{2,1,0:T(8,128)(2,1)S(1)} %copy-done, bf16[4,192,256]{2,1,0:T(8,128)(2,1)S(1)} %collective-permute-done.7.refs_3_, ...), custom_call_target="tpu_custom_call" | custom-call | flops 1811939328 | bytes 1048576 | tf_op jit(solution)/shard_map/attend/pallas_call | solution.py:183
  43.8 0.8 collective-permute-start.11
  44.6 0.5 collective-permute-done.12.refs_7_
  45.1 2.8 %collective-permute-start.14 = (bf16[2,4,96,256]{3,2,1,0:T(8,128)(2,1)S(1)}, bf16[2,4,96,256]{3,2,1,0:T(8,128)(2,1)S(1)}, u32[]{:S(2)}, u32[]{:S(2)}) collective-permute-start(bf16[2,4,96,256]{3,2,1,0:T(8,128)(2,1)S(1)} %collective-permute-done.12.refs_7_), channel_id=1, source_target_pairs={{0,4},{1,33},{4,8},{5,37},{8,12},{9,41},{12,0},{13,45},{16,20},{17... | collective-permute-start | bytes 1179656 | tf_op jit(solution)/shard_map/ppermute | solution.py:259
  47.9 6.1 %attend.6 = (f32[2,4,384,256]{3,2,1,0:T(8,128)S(1)}, f32[2,4,384,128]{3,2,1,0:T(8,128)S(1)}) custom-call(s32[4]{0:T(128)S(1)} %copy-done.1, f32[1,512]{1,0:T(1,128)S(1)} %bitcast.9, bf16[4,192,256]{2,1,0:T(8,128)(2,1)S(1)} %copy-done, bf16[4,192,256]{2,1,0:T(8,128)(2,1)S(1)} %collective-permute-done.7.refs_3_, ...), custom_call_target="tpu_custom_call" | custom-call | flops 3623878656 | bytes 1048576 | tf_op jit(solution)/shard_map/attend/pallas_call | solution.py:183
  54.1 0.9 collective-permute-done.14.refs_7_
  55.0 1.7 %collective-permute-start.15 = (bf16[2,4,96,256]{3,2,1,0:T(8,128)(2,1)S(1)}, bf16[2,4,96,256]{3,2,1,0:T(8,128)(2,1)S(1)}, u32[]{:S(2)}, u32[]{:S(2)}) collective-permute-start(bf16[2,4,96,256]{3,2,1,0:T(8,128)(2,1)S(1)} %collective-permute-done.14.refs_7_), channel_id=1, source_target_pairs={{0,4},{1,33},{4,8},{5,37},{8,12},{9,41},{12,0},{13,45},{16,20},{17... | collective-permute-start | bytes 1179656 | tf_op jit(solution)/shard_map/ppermute | solution.py:259
  56.6 6.1 %attend.7 = (f32[2,4,384,256]{3,2,1,0:T(8,128)S(1)}, f32[2,4,384,128]{3,2,1,0:T(8,128)S(1)}) custom-call(s32[4]{0:T(128)S(1)} %copy-done.1, f32[1,512]{1,0:T(1,128)S(1)} %bitcast.10, bf16[4,192,256]{2,1,0:T(8,128)(2,1)S(1)} %copy-done, bf16[4,192,256]{2,1,0:T(8,128)(2,1)S(1)} %collective-permute-done.7.refs_3_, ...), custom_call_target="tpu_custom_call" | custom-call | flops 3623878656 | bytes 1048576 | tf_op jit(solution)/shard_map/attend/pallas_call | solution.py:183
  62.7 0.5 collective-permute-start.16
  63.3 2.0 %collective-permute-done.15.refs_7_ = bf16[2,4,96,256]{3,2,1,0:T(8,128)(2,1)S(1)} collective-permute-done((bf16[2,4,96,256]{3,2,1,0:T(8,128)(2,1)S(1)}, bf16[2,4,96,256]{3,2,1,0:T(8,128)(2,1)S(1)}, u32[]{:S(2)}, u32[]{:S(2)}) %collective-permute-start.15) | collective-permute-done | bytes 393248 | tf_op jit(solution)/shard_map/ppermute | solution.py:259
  65.2 6.1 %attend.8 = (f32[2,4,384,256]{3,2,1,0:T(8,128)S(1)}, f32[2,4,384,128]{3,2,1,0:T(8,128)S(1)}) custom-call(s32[4]{0:T(128)S(1)} %copy-done.1, f32[1,512]{1,0:T(1,128)S(1)} %bitcast.11, bf16[4,192,256]{2,1,0:T(8,128)(2,1)S(1)} %copy-done, bf16[4,192,256]{2,1,0:T(8,128)(2,1)S(1)} %collective-permute-done.7.refs_3_, ...), custom_call_target="tpu_custom_call" | custom-call | flops 3623878656 | bytes 1048576 | tf_op jit(solution)/shard_map/attend/pallas_call | solution.py:183
  71.3 4.9 %attend.9 = (bf16[128,896]{1,0:T(8,128)(2,1)S(1)}, bf16[128,896]{1,0:T(8,128)(2,1)S(1)}, bf16[128,896]{1,0:T(8,128)(2,1)S(1)}, bf16[128,896]{1,0:T(8,128)(2,1)S(1)}) custom-call(s32[4]{0:T(128)S(1)} %copy-done.1, f32[1,256]{1,0:T(1,128)S(1)} %bitcast.12, bf16[4,192,256]{2,1,0:T(8,128)(2,1)S(1)} %copy-done, ...), custom_call_target="tpu_custom_call" | custom-call | flops 1811939328 | bytes 1048576 | tf_op jit(solution)/shard_map/attend/pallas_call | solution.py:183
  76.2 6.7 %collective-permute-start.17 = (bf16[128,896]{1,0:T(8,128)(2,1)S(1)}, bf16[128,896]{1,0:T(8,128)(2,1)S(1)}, u32[]{:S(2)}, u32[]{:S(2)}) collective-permute-start(bf16[128,896]{1,0:T(8,128)(2,1)S(1)} %get-tuple-element.75), channel_id=1, source_target_pairs={{0,0},{128,1},{1,64},{129,65},{64,128},{192,129},{65,192},{193,193... | collective-permute-start | bytes 688136 | tf_op jit(solution)/shard_map/ppermute | solution.py:329
  82.9 1.0 %collective-permute-start.19 = (bf16[128,896]{1,0:T(8,128)(2,1)S(1)}, bf16[128,896]{1,0:T(8,128)(2,1)S(1)}, u32[]{:S(2)}, u32[]{:S(2)}) collective-permute-start(bf16[128,896]{1,0:T(8,128)(2,1)S(1)} %get-tuple-element.77), channel_id=1, source_target_pairs={{64,0},{192,1},{65,64},{193,65},{0,128},{128,129},{1,192},{129,193... | collective-permute-start | bytes 688136 | tf_op jit(solution)/shard_map/ppermute | solution.py:329
  84.0 4.4 %collective-permute-start.20 = (bf16[128,896]{1,0:T(8,128)(2,1)S(1)}, bf16[128,896]{1,0:T(8,128)(2,1)S(1)}, u32[]{:S(2)}, u32[]{:S(2)}) collective-permute-start(bf16[128,896]{1,0:T(8,128)(2,1)S(1)} %get-tuple-element.78), channel_id=1, source_target_pairs={{65,0},{193,1},{64,64},{192,65},{1,128},{129,129},{0,192},{128,193... | collective-permute-start | bytes 688136 | tf_op jit(solution)/shard_map/ppermute | solution.py:329
  88.4 0.5 collective-permute-done.17.refs_0_
  88.9 1.5 %collective-permute-done.18.refs_1_ = bf16[128,896]{1,0:T(8,128)(2,1)S(1)} collective-permute-done((bf16[128,896]{1,0:T(8,128)(2,1)S(1)}, bf16[128,896]{1,0:T(8,128)(2,1)S(1)}, u32[]{:S(2)}, u32[]{:S(2)}) %collective-permute-start.18) | collective-permute-done | bytes 229408 | tf_op jit(solution)/shard_map/ppermute | solution.py:329
  90.4 4.7 %collective-permute-done.19.refs_2_ = bf16[128,896]{1,0:T(8,128)(2,1)S(1)} collective-permute-done((bf16[128,896]{1,0:T(8,128)(2,1)S(1)}, bf16[128,896]{1,0:T(8,128)(2,1)S(1)}, u32[]{:S(2)}, u32[]{:S(2)}) %collective-permute-start.19) | collective-permute-done | bytes 229408 | tf_op jit(solution)/shard_map/ppermute | solution.py:329
  95.1 0.1 collective-permute-done.20.refs_3_
  95.2 0.6 copy-done.5
  95.8 0.7 copy-done.6
  96.5 2.6 %merge.1 = bf16[128,1536]{1,0:T(8,128)(2,1)} custom-call(bf16[128,896]{1,0:T(8,128)(2,1)} %copy-done.3, bf16[128,896]{1,0:T(8,128)(2,1)} %copy-done.4, bf16[128,896]{1,0:T(8,128)(2,1)} %copy-done.5, bf16[128,896]{1,0:T(8,128)(2,1)} %copy-done.6), custom_call_target="tpu_custom_call" | custom-call | tf_op jit(solution)/shard_map/merge/pallas_call | solution.py:218
  (56 shorter events, 1.0 us)
Async XLA Ops:
  0.7 10.8 %collective-permute-start.3 = (bf16[32,512]{1,0:T(8,128)(2,1)S(1)}, bf16[32,512]{1,0:T(8,128)(2,1)S(1)}, u32[]{:S(2)}, u32[]{:S(2)}) collective-permute-start(bf16[32,512]{1,0:T(8,128)(2,1)S(1)} %pad_maximum_fusion.2), channel_id=1, source_target_pairs={{0,2},{2,0},{1,3},{3,1},{4,6},{6,4},{5,7},{7,5},{8,10},{10,8},{9,1... | collective-permute-start | bytes 98312 | tf_op jit(solution)/shard_map/ppermute | solution.py:233
  8.5 3.1 %collective-permute-start = (bf16[128,1536]{1,0:T(8,128)(2,1)}, bf16[128,1536]{1,0:T(8,128)(2,1)S(1)}, u32[]{:S(2)}, u32[]{:S(2)}) collective-permute-start(bf16[128,1536]{1,0:T(8,128)(2,1)} %q_ref.1), channel_id=1, source_target_pairs={{0,1},{1,0},{2,3},{3,2},{4,5},{5,4},{6,7},{7,6},{8,9},{9,8},{10,11... | collective-permute-start | bytes 1179656 | tf_op jit(solution)/shard_map/ppermute | solution.py:233
  9.4 2.1 %collective-permute-start.1 = (bf16[128,256]{1,0:T(8,128)(2,1)}, bf16[128,256]{1,0:T(8,128)(2,1)S(1)}, u32[]{:S(2)}, u32[]{:S(2)}) collective-permute-start(bf16[128,256]{1,0:T(8,128)(2,1)} %k_ref.1), channel_id=1, source_target_pairs={{0,1},{1,0},{2,3},{3,2},{4,5},{5,4},{6,7},{7,6},{8,9},{9,8},{10,11... | collective-permute-start | bytes 196616 | tf_op jit(solution)/shard_map/ppermute | solution.py:233
  9.4 2.1 %collective-permute-start.2 = (bf16[128,256]{1,0:T(8,128)(2,1)}, bf16[128,256]{1,0:T(8,128)(2,1)S(1)}, u32[]{:S(2)}, u32[]{:S(2)}) collective-permute-start(bf16[128,256]{1,0:T(8,128)(2,1)} %v_ref.1), channel_id=1, source_target_pairs={{0,1},{1,0},{2,3},{3,2},{4,5},{5,4},{6,7},{7,6},{8,9},{9,8},{10,11... | collective-permute-start | bytes 196616 | tf_op jit(solution)/shard_map/ppermute | solution.py:233
  11.5 0.6 copy-start.12
  11.5 0.6 copy-start.10
  11.5 0.6 copy-start.11
  12.2 0.7 copy-start.2
  15.0 6.5 %collective-permute-start.4 = (bf16[288,256]{1,0:T(8,128)(2,1)}, bf16[288,256]{1,0:T(8,128)(2,1)S(1)}, u32[]{:S(2)}, u32[]{:S(2)}) collective-permute-start(bf16[288,256]{1,0:T(8,128)(2,1)} %get-tuple-element.43), channel_id=1, source_target_pairs={{0,64},{64,128},{128,192},{192,0},{1,65},{65,129},{129,193},{193,1... | collective-permute-start | bytes 442376 | tf_op jit(solution)/shard_map/ppermute | solution.py:233
  16.3 9.8 %collective-permute-start.5 = (bf16[288,256]{1,0:T(8,128)(2,1)}, bf16[288,256]{1,0:T(8,128)(2,1)S(1)}, u32[]{:S(2)}, u32[]{:S(2)}) collective-permute-start(bf16[288,256]{1,0:T(8,128)(2,1)} %get-tuple-element.44), channel_id=1, source_target_pairs={{0,128},{64,192},{128,0},{192,64},{1,129},{65,193},{129,1},{193,65... | collective-permute-start | bytes 442376 | tf_op jit(solution)/shard_map/ppermute | solution.py:233
  18.7 7.4 %collective-permute-start.6 = (bf16[288,256]{1,0:T(8,128)(2,1)}, bf16[288,256]{1,0:T(8,128)(2,1)S(1)}, u32[]{:S(2)}, u32[]{:S(2)}) collective-permute-start(bf16[288,256]{1,0:T(8,128)(2,1)} %get-tuple-element.45), channel_id=1, source_target_pairs={{0,192},{64,0},{128,64},{192,128},{1,193},{65,1},{129,65},{193,129... | collective-permute-start | bytes 442376 | tf_op jit(solution)/shard_map/ppermute | solution.py:233
  21.6 4.5 %copy-start.7 = (bf16[288,256]{1,0:T(8,128)(2,1)}, bf16[288,256]{1,0:T(8,128)(2,1)S(1)}, u32[]{:S(2)}) copy-start(bf16[288,256]{1,0:T(8,128)(2,1)S(1)} %collective-permute-done.4.refs_1_) | copy-start | bytes 442372
  26.1 0.7 copy-start.8
  26.1 0.7 copy-start.9
  28.8 9.5 %collective-permute-start.7 = (bf16[4,192,256]{2,1,0:T(8,128)(2,1)}, bf16[4,192,256]{2,1,0:T(8,128)(2,1)S(1)}, u32[]{:S(2)}, u32[]{:S(2)}) collective-permute-start(bf16[4,192,256]{2,1,0:T(8,128)(2,1)} %get-tuple-element.46.refs_2_), channel_id=1, source_target_pairs={{0,1},{1,0},{2,3},{3,2},{4,5},{5,4},{6,7},{7,6},{8,9},{9,8},{10,11... | collective-permute-start | bytes 1179656 | tf_op jit(solution)/shard_map/ppermute | solution.py:233
  29.7 6.2 %collective-permute-start.9 = (bf16[4,96,256]{2,1,0:T(8,128)(2,1)}, bf16[4,96,256]{2,1,0:T(8,128)(2,1)S(1)}, u32[]{:S(2)}, u32[]{:S(2)}) collective-permute-start(bf16[4,96,256]{2,1,0:T(8,128)(2,1)} %get-tuple-element.47), channel_id=1, source_target_pairs={{0,32},{1,5},{4,36},{5,9},{8,40},{9,13},{12,44},{13,1},{16,0},{17,... | collective-permute-start | bytes 589832 | tf_op jit(solution)/shard_map/ppermute | solution.py:259
  31.0 12.6 %collective-permute-start.8 = (bf16[4,96,256]{2,1,0:T(8,128)(2,1)}, bf16[4,96,256]{2,1,0:T(8,128)(2,1)S(1)}, u32[]{:S(2)}, u32[]{:S(2)}) collective-permute-start(bf16[4,96,256]{2,1,0:T(8,128)(2,1)} %get-tuple-element.47), channel_id=1, source_target_pairs={{0,16},{1,13},{4,20},{5,1},{8,24},{9,5},{12,28},{13,9},{16,48},{17... | collective-permute-start | bytes 589832 | tf_op jit(solution)/shard_map/ppermute | solution.py:259
  35.9 7.8 %collective-permute-start.10 = (bf16[4,96,256]{2,1,0:T(8,128)(2,1)S(1)}, bf16[4,96,256]{2,1,0:T(8,128)(2,1)S(1)}, u32[]{:S(2)}, u32[]{:S(2)}) collective-permute-start(bf16[4,96,256]{2,1,0:T(8,128)(2,1)S(1)} %collective-permute-done.9), channel_id=1, source_target_pairs={{0,32},{1,5},{4,36},{5,9},{8,40},{9,13},{12,44},{13,1},{16,0},{17,... | collective-permute-start | bytes 589832 | tf_op jit(solution)/shard_map/ppermute | solution.py:259
  37.0 8.1 %collective-permute-start.12 = (bf16[2,4,96,256]{3,2,1,0:T(8,128)(2,1)S(1)}, bf16[2,4,96,256]{3,2,1,0:T(8,128)(2,1)S(1)}, u32[]{:S(2)}, u32[]{:S(2)}) collective-permute-start(bf16[2,4,96,256]{3,2,1,0:T(8,128)(2,1)S(1)} %pad_maximum_fusion.refs_4_), channel_id=1, source_target_pairs={{0,4},{1,33},{4,8},{5,37},{8,12},{9,41},{12,0},{13,45},{16,20},{17... | collective-permute-start | bytes 1179656 | tf_op jit(solution)/shard_map/ppermute | solution.py:259
  38.3 1.0 %copy-start = (bf16[4,192,256]{2,1,0:T(8,128)(2,1)S(1)}, bf16[4,192,256]{2,1,0:T(8,128)(2,1)}, u32[]{:S(2)}) copy-start(bf16[4,192,256]{2,1,0:T(8,128)(2,1)} %get-tuple-element.46.refs_2_) | copy-start | bytes 1179652
  39.3 0.7 copy-start.1
  43.8 10.2 %collective-permute-start.11 = (bf16[2,4,96,256]{3,2,1,0:T(8,128)(2,1)S(1)}, bf16[2,4,96,256]{3,2,1,0:T(8,128)(2,1)S(1)}, u32[]{:S(2)}, u32[]{:S(2)}) collective-permute-start(bf16[2,4,96,256]{3,2,1,0:T(8,128)(2,1)S(1)} %pad_maximum_fusion.1.refs_6_), channel_id=1, source_target_pairs={{0,4},{1,33},{4,8},{5,37},{8,12},{9,41},{12,0},{13,45},{16,20},{17... | collective-permute-start | bytes 1179656 | tf_op jit(solution)/shard_map/ppermute | solution.py:259
  45.1 9.8 %collective-permute-start.14 = (bf16[2,4,96,256]{3,2,1,0:T(8,128)(2,1)S(1)}, bf16[2,4,96,256]{3,2,1,0:T(8,128)(2,1)S(1)}, u32[]{:S(2)}, u32[]{:S(2)}) collective-permute-start(bf16[2,4,96,256]{3,2,1,0:T(8,128)(2,1)S(1)} %collective-permute-done.12.refs_7_), channel_id=1, source_target_pairs={{0,4},{1,33},{4,8},{5,37},{8,12},{9,41},{12,0},{13,45},{16,20},{17... | collective-permute-start | bytes 1179656 | tf_op jit(solution)/shard_map/ppermute | solution.py:259
  54.0 8.7 %collective-permute-start.13 = (bf16[2,4,96,256]{3,2,1,0:T(8,128)(2,1)S(1)}, bf16[2,4,96,256]{3,2,1,0:T(8,128)(2,1)S(1)}, u32[]{:S(2)}, u32[]{:S(2)}) collective-permute-start(bf16[2,4,96,256]{3,2,1,0:T(8,128)(2,1)S(1)} %collective-permute-done.11.refs_6_), channel_id=1, source_target_pairs={{0,4},{1,33},{4,8},{5,37},{8,12},{9,41},{12,0},{13,45},{16,20},{17... | collective-permute-start | bytes 1179656 | tf_op jit(solution)/shard_map/ppermute | solution.py:259
  55.0 10.3 %collective-permute-start.15 = (bf16[2,4,96,256]{3,2,1,0:T(8,128)(2,1)S(1)}, bf16[2,4,96,256]{3,2,1,0:T(8,128)(2,1)S(1)}, u32[]{:S(2)}, u32[]{:S(2)}) collective-permute-start(bf16[2,4,96,256]{3,2,1,0:T(8,128)(2,1)S(1)} %collective-permute-done.14.refs_7_), channel_id=1, source_target_pairs={{0,4},{1,33},{4,8},{5,37},{8,12},{9,41},{12,0},{13,45},{16,20},{17... | collective-permute-start | bytes 1179656 | tf_op jit(solution)/shard_map/ppermute | solution.py:259
  62.7 8.6 %collective-permute-start.16 = (bf16[2,4,96,256]{3,2,1,0:T(8,128)(2,1)S(1)}, bf16[2,4,96,256]{3,2,1,0:T(8,128)(2,1)S(1)}, u32[]{:S(2)}, u32[]{:S(2)}) collective-permute-start(bf16[2,4,96,256]{3,2,1,0:T(8,128)(2,1)S(1)} %collective-permute-done.13.refs_6_), channel_id=1, source_target_pairs={{0,4},{1,33},{4,8},{5,37},{8,12},{9,41},{12,0},{13,45},{16,20},{17... | collective-permute-start | bytes 1179656 | tf_op jit(solution)/shard_map/ppermute | solution.py:259
  76.2 12.7 %collective-permute-start.17 = (bf16[128,896]{1,0:T(8,128)(2,1)S(1)}, bf16[128,896]{1,0:T(8,128)(2,1)S(1)}, u32[]{:S(2)}, u32[]{:S(2)}) collective-permute-start(bf16[128,896]{1,0:T(8,128)(2,1)S(1)} %get-tuple-element.75), channel_id=1, source_target_pairs={{0,0},{128,1},{1,64},{129,65},{64,128},{192,129},{65,192},{193,193... | collective-permute-start | bytes 688136 | tf_op jit(solution)/shard_map/ppermute | solution.py:329
  82.8 7.6 %collective-permute-start.18 = (bf16[128,896]{1,0:T(8,128)(2,1)S(1)}, bf16[128,896]{1,0:T(8,128)(2,1)S(1)}, u32[]{:S(2)}, u32[]{:S(2)}) collective-permute-start(bf16[128,896]{1,0:T(8,128)(2,1)S(1)} %get-tuple-element.76), channel_id=1, source_target_pairs={{1,0},{129,1},{0,64},{128,65},{65,128},{193,129},{64,192},{192,193... | collective-permute-start | bytes 688136 | tf_op jit(solution)/shard_map/ppermute | solution.py:329
  82.9 12.2 %collective-permute-start.19 = (bf16[128,896]{1,0:T(8,128)(2,1)S(1)}, bf16[128,896]{1,0:T(8,128)(2,1)S(1)}, u32[]{:S(2)}, u32[]{:S(2)}) collective-permute-start(bf16[128,896]{1,0:T(8,128)(2,1)S(1)} %get-tuple-element.77), channel_id=1, source_target_pairs={{64,0},{192,1},{65,64},{193,65},{0,128},{128,129},{1,192},{129,193... | collective-permute-start | bytes 688136 | tf_op jit(solution)/shard_map/ppermute | solution.py:329
  84.0 11.3 %collective-permute-start.20 = (bf16[128,896]{1,0:T(8,128)(2,1)S(1)}, bf16[128,896]{1,0:T(8,128)(2,1)S(1)}, u32[]{:S(2)}, u32[]{:S(2)}) collective-permute-start(bf16[128,896]{1,0:T(8,128)(2,1)S(1)} %get-tuple-element.78), channel_id=1, source_target_pairs={{65,0},{193,1},{64,64},{192,65},{1,128},{129,129},{0,192},{128,193... | collective-permute-start | bytes 688136 | tf_op jit(solution)/shard_map/ppermute | solution.py:329
  88.9 6.3 %copy-start.3 = (bf16[128,896]{1,0:T(8,128)(2,1)}, bf16[128,896]{1,0:T(8,128)(2,1)S(1)}, u32[]{:S(2)}) copy-start(bf16[128,896]{1,0:T(8,128)(2,1)S(1)} %collective-permute-done.17.refs_0_) | copy-start | bytes 688132
  90.4 4.8 %copy-start.4 = (bf16[128,896]{1,0:T(8,128)(2,1)}, bf16[128,896]{1,0:T(8,128)(2,1)S(1)}, u32[]{:S(2)}) copy-start(bf16[128,896]{1,0:T(8,128)(2,1)S(1)} %collective-permute-done.18.refs_1_) | copy-start | bytes 688132
  95.1 0.7 copy-start.5
  95.8 0.7 copy-start.6
where the time goes:
time: 99.4 us; the launch traced here: 99.1 us
  starting transfers between devices  37.3 us (38%)
  Pallas kernels  33.5 us (34%)
  waiting for transfers between devices  19.7 us (20%)
  local copies, waits for them, and re-layouts  6.92 us (7%)
  other arithmetic  1.45 us (1%)
    pallas_call x5, Pallas kernels, attend(): pl.pallas_call(lambda *refs: attend_body(state is None, last, refs), in_s...  26.8 us
    ppermute x8, starting transfers between devices, shift(): lax.ppermute(array, axis, [(i, (i + by) % size) for i in range(size)])  14.8 us
    ppermute x4, starting transfers between devices, on_device(): lax.ppermute(state[s], ('x', 'core'), [(b, a) for a, b in spread(s)])  12.2 us
    ppermute x9, starting transfers between devices, step_on(): return lax.ppermute(block, ('zl', 'y', 'core'), pairs)  10.2 us
    ppermute x4, waiting for transfers between devices, on_device(): lax.ppermute(state[s], ('x', 'core'), [(b, a) for a, b in spread(s)])  6.81 us
    ppermute x9, waiting for transfers between devices, step_on(): return lax.ppermute(block, ('zl', 'y', 'core'), pairs)  6.68 us
    ppermute x8, waiting for transfers between devices, shift(): lax.ppermute(array, axis, [(i, (i + by) % size) for i in range(size)])  6.24 us
    unnamed x26, local copies, waits for them, and re-layouts  5.04 us
  transfers between devices with their start and end apart: 21, of which 10 were waited for; matrix products, arithmetic and copies ran while one was open for 3% of the time, Pallas kernels for 22%

commit v1 on v0

--- a/solution.py
+++ b/solution.py
@@ -23,6 +23,9 @@
 smem = pl.BlockSpec(memory_space=pltpu.SMEM)
 
 
+small = pltpu.CompilerParams(vmem_limit_bytes=8 * 2**20)
+
+
 def shaped(shape, dtype=BF):
     return jax.ShapeDtypeStruct(shape, dtype)
 
@@ -35,40 +38,69 @@
     return pl.ds(pl.multiple_of(index * step, step), step)
 
 
-def deal_body(q_ref, k_ref, v_ref, ck_ref, cv_ref, q_got, k_got, v_got, c_got, *outs):
+def from_one_core(head, q, k, v, out):
+    rows, e = aligned(lax.axis_index("core"), HALF), head & 1
+    out[:HALF, :D] = k[rows, aligned(e, D)]
+    out[:HALF, D:] = v[rows, aligned(e, D)]
+    for i in range(3):
+        lanes = pl.ds(pl.multiple_of(e * WIDE + i * 2 * D, D), 2 * D)
+        out[BLOCK + i * HALF : BLOCK + (i + 1) * HALF, :] = q[rows, lanes]
+
+
+def deal_body(q_ref, k_ref, v_ref, ck_ref, cv_ref, *outs):
     x, half, core = lax.axis_index("x"), lax.axis_index("zh"), lax.axis_index("core")
-    rows = aligned(core, HALF)
     for s in range(4):
-        head = (x + s) & 3
-        out = outs[s]
-
-        def from_core(q, k, v, out=out, e=head & 1):
-            out[:HALF, :D] = k[rows, aligned(e, D)]
-            out[:HALF, D:] = v[rows, aligned(e, D)]
-            for i in range(3):
-                lanes = pl.ds(pl.multiple_of(e * WIDE + i * 2 * D, D), 2 * D)
-                out[BLOCK + i * HALF : BLOCK + (i + 1) * HALF, :] = q[rows, lanes]
+        head, out = (x + s) & 3, outs[s]
 
         @pl.when((head >> 1) == core)
-        def _():
-            from_core(q_ref, k_ref, v_ref)
-
-        @pl.when((head >> 1) != core)
-        def _():
-            from_core(q_got, k_got, v_got)
+        def _(head=head, out=out):
+            from_one_core(head, q_ref, k_ref, v_ref, out)
 
         lanes = aligned(half * 4 + head, D)
         out[HALF : HALF + 16, :D] = ck_ref[:, lanes]
         out[HALF : HALF + 16, D:] = cv_ref[:, lanes]
+
+
+def deal(*own):
+    return pl.pallas_call(
+        deal_body,
+        in_specs=[vmem] * len(own),
+        out_specs=[vmem] * 4,
+        out_shape=[shaped((MESSAGE, 2 * D))] * 4,
+        compiler_params=small,
+        name="deal",
+    )(*own)
+
+
+def fill_body(q_got, k_got, v_got, c_got, *refs):
+    x, core = lax.axis_index("x"), lax.axis_index("core")
+    for s in range(4):
+        head, mine, out = (x + s) & 3, refs[s], refs[4 + s]
+
+        @pl.when((head >> 1) == core)
+        def _(mine=mine, out=out):
+            out[:HALF, :] = mine[:HALF, :]
+            out[BLOCK:, :] = mine[BLOCK:, :]
+
+        @pl.when((head >> 1) != core)
+        def _(head=head, out=out):
+            from_one_core(head, q_got, k_got, v_got, out)
+
         lanes = aligned(head, D)
+        out[HALF : HALF + 16, :] = mine[HALF : HALF + 16, :]
         out[HALF + 16 : BLOCK, :D] = c_got[:16, lanes]
         out[HALF + 16 : BLOCK, D:] = c_got[16:, lanes]
 
 
-def deal(own, got):
-    return pl.pallas_call(
-        deal_body, out_shape=[shaped((MESSAGE, 2 * D))] * 4, name="deal"
-    )(*own, *got)
+def fill(got, messages):
+    return pl.pallas_call(
+        fill_body,
+        in_specs=[vmem] * 8,
+        out_specs=[vmem] * 4,
+        out_shape=[shaped((MESSAGE, 2 * D))] * 4,
+        compiler_params=small,
+        name="fill",
+    )(*got, *messages)
 
 
 def join_body(*refs):
@@ -83,7 +115,10 @@
 def join(messages):
     return pl.pallas_call(
         join_body,
+        in_specs=[vmem] * 4,
+        out_specs=[vmem] * 2,
         out_shape=[shaped((4, BLOCK, 2 * D)), shaped((4, 3 * HALF, 2 * D))],
+        compiler_params=small,
         name="join",
     )(*messages)
 
@@ -216,7 +251,12 @@
 
 def merge(messages):
     return pl.pallas_call(
-        merge_body, out_shape=shaped((2 * HALF, 2 * WIDE)), name="merge"
+        merge_body,
+        in_specs=[vmem] * 4,
+        out_specs=vmem,
+        out_shape=shaped((2 * HALF, 2 * WIDE)),
+        compiler_params=small,
+        name="merge",
     )(*messages)
 
 
@@ -299,7 +339,7 @@
     start = 4 * D * (1 - lax.axis_index("zh"))
     halves = [lax.dynamic_slice_in_dim(c, start, 4 * D, 1) for c in (cache_keys, cache_values)]
     got.append(shift(jnp.concatenate(halves), "zh", 1, 2))
-    messages = deal((queries, keys, values, cache_keys, cache_values), got)
+    messages = fill(got, deal(queries, keys, values, cache_keys, cache_values))
     messages = [messages[0]] + [shift(messages[s], "x", s) for s in range(1, 4)]
     block, mine = join(messages)
     q = [mine, swap(mine)]

time: 99.4 us -> 92.9 us (0.935)
  Pallas kernels: 33.5 us -> 28.3 us
    pallas_call x3 -> x4, Pallas kernels: 6.68 us -> 1.48 us  [the longest x1 1.29 us: merge(): pl.pallas_call(merge_body, in_specs=[vmem] * 4, out_specs=vmem, out_shape...]
    ppermute x4, starting transfers between devices: 12.2 us -> 10.8 us  [on_device(): lax.ppermute(state[s], ('x', 'core'), [(b, a) for a, b in spread(s)])]
    ppermute x9, starting transfers between devices: 10.2 us -> 11.6 us  [step_on(): return lax.ppermute(block, ('zl', 'y', 'core'), pairs)]
    unnamed x26 -> x12, local copies, waits for them, and re-layouts: 5.04 us -> 4.19 us
  transfers between devices with their start and end apart: 21 -> 21, of which waited for: 10 -> 10; matrix products, arithmetic and copies ran while one was open for 3% -> 2% of each run, Pallas kernels for 22% -> 24%
where the time goes in v1:
time: 92.9 us; the launch traced here: 92.5 us
  starting transfers between devices  37.4 us (40%)
  Pallas kernels  28.3 us (30%)
  waiting for transfers between devices  19.9 us (21%)
  local copies, waits for them, and re-layouts  6.08 us (7%)
    pallas_call x5, Pallas kernels, attend(): pl.pallas_call(lambda *refs: attend_body(state is None, last, refs), in_s...  26.8 us
    ppermute x8, starting transfers between devices, shift(): lax.ppermute(array, axis, [(i, (i + by) % size) for i in range(size)])  15 us
    ppermute x9, starting transfers between devices, step_on(): return lax.ppermute(block, ('zl', 'y', 'core'), pairs)  11.6 us
    ppermute x4, starting transfers between devices, on_device(): lax.ppermute(state[s], ('x', 'core'), [(b, a) for a, b in spread(s)])  10.8 us
    ppermute x9, waiting for transfers between devices, step_on(): return lax.ppermute(block, ('zl', 'y', 'core'), pairs)  7.07 us
    ppermute x4, waiting for transfers between devices, on_device(): lax.ppermute(state[s], ('x', 'core'), [(b, a) for a, b in spread(s)])  6.85 us
    ppermute x8, waiting for transfers between devices, shift(): lax.ppermute(array, axis, [(i, (i + by) % size) for i in range(size)])  6.02 us
    unnamed x12, local copies, waits for them, and re-layouts  4.19 us
  transfers between devices with their start and end apart: 21, of which 10 were waited for; matrix products, arithmetic and copies ran while one was open for 2% of the time, Pallas kernels for 24%

profile of v1, /device:TPU:1, one launch (start us, length us, event | category | flops | bytes accessed | tf_op | source)
XLA Modules:
  0.0 92.5 jit_solution(1091064379954787999)
XLA Ops:
  0.0 0.7 constant_dynamic-slice_fusion
  0.8 7.7 %collective-permute-start.3 = (bf16[32,512]{1,0:T(8,128)(2,1)S(1)}, bf16[32,512]{1,0:T(8,128)(2,1)S(1)}, u32[]{:S(2)}, u32[]{:S(2)}) collective-permute-start(bf16[32,512]{1,0:T(8,128)(2,1)S(1)} %pad_maximum_fusion.2), channel_id=1, source_target_pairs={{0,2},{2,0},{1,3},{3,1},{4,6},{6,4},{5,7},{7,5},{8,10},{10,8},{9,1... | collective-permute-start | bytes 98312 | tf_op jit(solution)/shard_map/ppermute | solution.py:273
  8.5 1.0 %collective-permute-start = (bf16[128,1536]{1,0:T(8,128)(2,1)}, bf16[128,1536]{1,0:T(8,128)(2,1)S(1)}, u32[]{:S(2)}, u32[]{:S(2)}) collective-permute-start(bf16[128,1536]{1,0:T(8,128)(2,1)} %q_ref.1), channel_id=1, source_target_pairs={{0,1},{1,0},{2,3},{3,2},{4,5},{5,4},{6,7},{7,6},{8,9},{9,8},{10,11... | collective-permute-start | bytes 1179656 | tf_op jit(solution)/shard_map/ppermute | solution.py:273
  9.5 0.5 collective-permute-start.2
  10.1 0.1 multiply_add_fusion.1
  10.2 0.7 slice.2
  10.9 0.1 reshape.768
  11.1 0.1 reshape.770
  11.2 0.1 compare_reduce_fusion
  11.4 1.0 %copy-done = bf16[128,1536]{1,0:T(8,128)(2,1)S(1)} copy-done((bf16[128,1536]{1,0:T(8,128)(2,1)S(1)}, bf16[128,1536]{1,0:T(8,128)(2,1)}, u32[]{:S(2)}) %copy-start) | copy-done | bytes 393240
  12.3 0.8 copy-done.1
  13.1 0.8 copy-done.2
  13.9 0.8 copy-done.3
  14.7 0.8 copy-done.4
  15.8 0.1 fill.1
  15.9 1.3 %collective-permute-start.4 = (bf16[288,256]{1,0:T(8,128)(2,1)S(1)}, bf16[288,256]{1,0:T(8,128)(2,1)S(1)}, u32[]{:S(2)}, u32[]{:S(2)}) collective-permute-start(bf16[288,256]{1,0:T(8,128)(2,1)S(1)} %get-tuple-element.51), channel_id=1, source_target_pairs={{0,64},{64,128},{128,192},{192,0},{1,65},{65,129},{129,193},{193,1... | collective-permute-start | bytes 442376 | tf_op jit(solution)/shard_map/ppermute | solution.py:273
  17.2 2.5 %collective-permute-start.5 = (bf16[288,256]{1,0:T(8,128)(2,1)S(1)}, bf16[288,256]{1,0:T(8,128)(2,1)S(1)}, u32[]{:S(2)}, u32[]{:S(2)}) collective-permute-start(bf16[288,256]{1,0:T(8,128)(2,1)S(1)} %get-tuple-element.52), channel_id=1, source_target_pairs={{0,128},{64,192},{128,0},{192,64},{1,129},{65,193},{129,1},{193,65... | collective-permute-start | bytes 442376 | tf_op jit(solution)/shard_map/ppermute | solution.py:273
  19.6 1.2 %collective-permute-start.6 = (bf16[288,256]{1,0:T(8,128)(2,1)S(1)}, bf16[288,256]{1,0:T(8,128)(2,1)S(1)}, u32[]{:S(2)}, u32[]{:S(2)}) collective-permute-start(bf16[288,256]{1,0:T(8,128)(2,1)S(1)} %get-tuple-element.53), channel_id=1, source_target_pairs={{0,192},{64,0},{128,64},{192,128},{1,193},{65,1},{129,65},{193,129... | collective-permute-start | bytes 442376 | tf_op jit(solution)/shard_map/ppermute | solution.py:273
  20.8 1.9 %collective-permute-done.4.refs_1_ = bf16[288,256]{1,0:T(8,128)(2,1)S(1)} collective-permute-done((bf16[288,256]{1,0:T(8,128)(2,1)S(1)}, bf16[288,256]{1,0:T(8,128)(2,1)S(1)}, u32[]{:S(2)}, u32[]{:S(2)}) %collective-permute-start.4) | collective-permute-done | bytes 147488 | tf_op jit(solution)/shard_map/ppermute | solution.py:273
  22.6 4.2 %collective-permute-done.5.refs_2_ = bf16[288,256]{1,0:T(8,128)(2,1)S(1)} collective-permute-done((bf16[288,256]{1,0:T(8,128)(2,1)S(1)}, bf16[288,256]{1,0:T(8,128)(2,1)S(1)}, u32[]{:S(2)}, u32[]{:S(2)}) %collective-permute-start.5) | collective-permute-done | bytes 147488 | tf_op jit(solution)/shard_map/ppermute | solution.py:273
  26.9 0.9 collective-permute-start.7
  27.7 0.1 compare_reduce_fusion.3
  27.8 1.4 %collective-permute-start.9 = (bf16[4,96,256]{2,1,0:T(8,128)(2,1)S(1)}, bf16[4,96,256]{2,1,0:T(8,128)(2,1)S(1)}, u32[]{:S(2)}, u32[]{:S(2)}) collective-permute-start(bf16[4,96,256]{2,1,0:T(8,128)(2,1)S(1)} %get-tuple-element.55), channel_id=1, source_target_pairs={{0,32},{1,5},{4,36},{5,9},{8,40},{9,13},{12,44},{13,1},{16,0},{17,... | collective-permute-start | bytes 589832 | tf_op jit(solution)/shard_map/ppermute | solution.py:299
  29.2 1.5 %collective-permute-start.8 = (bf16[4,96,256]{2,1,0:T(8,128)(2,1)S(1)}, bf16[4,96,256]{2,1,0:T(8,128)(2,1)S(1)}, u32[]{:S(2)}, u32[]{:S(2)}) collective-permute-start(bf16[4,96,256]{2,1,0:T(8,128)(2,1)S(1)} %get-tuple-element.55), channel_id=1, source_target_pairs={{0,16},{1,13},{4,20},{5,1},{8,24},{9,5},{12,28},{13,9},{16,48},{17... | collective-permute-start | bytes 589832 | tf_op jit(solution)/shard_map/ppermute | solution.py:299
  30.7 3.1 %collective-permute-done.9 = bf16[4,96,256]{2,1,0:T(8,128)(2,1)S(1)} collective-permute-done((bf16[4,96,256]{2,1,0:T(8,128)(2,1)S(1)}, bf16[4,96,256]{2,1,0:T(8,128)(2,1)S(1)}, u32[]{:S(2)}, u32[]{:S(2)}) %collective-permute-start.9) | collective-permute-done | bytes 196640 | tf_op jit(solution)/shard_map/ppermute | solution.py:299
  33.8 0.2 collective-permute-start.10
  34.1 1.3 %collective-permute-start.12 = (bf16[2,4,96,256]{3,2,1,0:T(8,128)(2,1)S(1)}, bf16[2,4,96,256]{3,2,1,0:T(8,128)(2,1)S(1)}, u32[]{:S(2)}, u32[]{:S(2)}) collective-permute-start(bf16[2,4,96,256]{3,2,1,0:T(8,128)(2,1)S(1)} %pad_maximum_fusion.refs_4_), channel_id=1, source_target_pairs={{0,4},{1,33},{4,8},{5,37},{8,12},{9,41},{12,0},{13,45},{16,20},{17... | collective-permute-start | bytes 1179656 | tf_op jit(solution)/shard_map/ppermute | solution.py:299
  35.3 3.7 %attend.5 = (f32[2,4,384,256]{3,2,1,0:T(8,128)S(1)}, f32[2,4,384,128]{3,2,1,0:T(8,128)S(1)}) custom-call(s32[4]{0:T(128)S(1)} %copy-done.5, f32[1,256]{1,0:T(1,128)S(1)} %bitcast.14, bf16[4,192,256]{2,1,0:T(8,128)(2,1)S(1)} %get-tuple-element.54.refs_2_, bf16[4,192,256]{2,1,0:T(8,128)(2,1)S(1)} %collective-permute-done.7.refs_3_, ...), custom_call_target="tpu_custom_call" | custom-call | flops 1811939328 | bytes 1048576 | tf_op jit(solution)/shard_map/attend/pallas_call | solution.py:218
  39.1 0.5 collective-permute-done.10
  39.6 2.3 %collective-permute-start.11 = (bf16[2,4,96,256]{3,2,1,0:T(8,128)(2,1)S(1)}, bf16[2,4,96,256]{3,2,1,0:T(8,128)(2,1)S(1)}, u32[]{:S(2)}, u32[]{:S(2)}) collective-permute-start(bf16[2,4,96,256]{3,2,1,0:T(8,128)(2,1)S(1)} %pad_maximum_fusion.1.refs_6_), channel_id=1, source_target_pairs={{0,4},{1,33},{4,8},{5,37},{8,12},{9,41},{12,0},{13,45},{16,20},{17... | collective-permute-start | bytes 1179656 | tf_op jit(solution)/shard_map/ppermute | solution.py:299
  41.9 1.2 %collective-permute-done.12.refs_7_ = bf16[2,4,96,256]{3,2,1,0:T(8,128)(2,1)S(1)} collective-permute-done((bf16[2,4,96,256]{3,2,1,0:T(8,128)(2,1)S(1)}, bf16[2,4,96,256]{3,2,1,0:T(8,128)(2,1)S(1)}, u32[]{:S(2)}, u32[]{:S(2)}) %collective-permute-start.12) | collective-permute-done | bytes 393248 | tf_op jit(solution)/shard_map/ppermute | solution.py:299
  43.1 2.2 %collective-permute-start.14 = (bf16[2,4,96,256]{3,2,1,0:T(8,128)(2,1)S(1)}, bf16[2,4,96,256]{3,2,1,0:T(8,128)(2,1)S(1)}, u32[]{:S(2)}, u32[]{:S(2)}) collective-permute-start(bf16[2,4,96,256]{3,2,1,0:T(8,128)(2,1)S(1)} %collective-permute-done.12.refs_7_), channel_id=1, source_target_pairs={{0,4},{1,33},{4,8},{5,37},{8,12},{9,41},{12,0},{13,45},{16,20},{17... | collective-permute-start | bytes 1179656 | tf_op jit(solution)/shard_map/ppermute | solution.py:299
  45.3 6.1 %attend.6 = (f32[2,4,384,256]{3,2,1,0:T(8,128)S(1)}, f32[2,4,384,128]{3,2,1,0:T(8,128)S(1)}) custom-call(s32[4]{0:T(128)S(1)} %copy-done.5, f32[1,512]{1,0:T(1,128)S(1)} %bitcast.10, bf16[4,192,256]{2,1,0:T(8,128)(2,1)S(1)} %get-tuple-element.54.refs_2_, bf16[4,192,256]{2,1,0:T(8,128)(2,1)S(1)} %collective-permute-done.7.refs_3_, ...), custom_call_target="tpu_custom_call" | custom-call | flops 3623878656 | bytes 1048576 | tf_op jit(solution)/shard_map/attend/pallas_call | solution.py:218
  51.5 2.4 %collective-permute-start.15 = (bf16[2,4,96,256]{3,2,1,0:T(8,128)(2,1)S(1)}, bf16[2,4,96,256]{3,2,1,0:T(8,128)(2,1)S(1)}, u32[]{:S(2)}, u32[]{:S(2)}) collective-permute-start(bf16[2,4,96,256]{3,2,1,0:T(8,128)(2,1)S(1)} %collective-permute-done.14.refs_7_), channel_id=1, source_target_pairs={{0,4},{1,33},{4,8},{5,37},{8,12},{9,41},{12,0},{13,45},{16,20},{17... | collective-permute-start | bytes 1179656 | tf_op jit(solution)/shard_map/ppermute | solution.py:299
  53.9 6.1 %attend.7 = (f32[2,4,384,256]{3,2,1,0:T(8,128)S(1)}, f32[2,4,384,128]{3,2,1,0:T(8,128)S(1)}) custom-call(s32[4]{0:T(128)S(1)} %copy-done.5, f32[1,512]{1,0:T(1,128)S(1)} %bitcast.11, bf16[4,192,256]{2,1,0:T(8,128)(2,1)S(1)} %get-tuple-element.54.refs_2_, bf16[4,192,256]{2,1,0:T(8,128)(2,1)S(1)} %collective-permute-done.7.refs_3_, ...), custom_call_target="tpu_custom_call" | custom-call | flops 3623878656 | bytes 1048576 | tf_op jit(solution)/shard_map/attend/pallas_call | solution.py:218
  60.0 0.3 collective-permute-start.16
  60.3 2.2 %collective-permute-done.15.refs_7_ = bf16[2,4,96,256]{3,2,1,0:T(8,128)(2,1)S(1)} collective-permute-done((bf16[2,4,96,256]{3,2,1,0:T(8,128)(2,1)S(1)}, bf16[2,4,96,256]{3,2,1,0:T(8,128)(2,1)S(1)}, u32[]{:S(2)}, u32[]{:S(2)}) %collective-permute-start.15) | collective-permute-done | bytes 393248 | tf_op jit(solution)/shard_map/ppermute | solution.py:299
  62.6 6.1 %attend.8 = (f32[2,4,384,256]{3,2,1,0:T(8,128)S(1)}, f32[2,4,384,128]{3,2,1,0:T(8,128)S(1)}) custom-call(s32[4]{0:T(128)S(1)} %copy-done.5, f32[1,512]{1,0:T(1,128)S(1)} %bitcast.12, bf16[4,192,256]{2,1,0:T(8,128)(2,1)S(1)} %get-tuple-element.54.refs_2_, bf16[4,192,256]{2,1,0:T(8,128)(2,1)S(1)} %collective-permute-done.7.refs_3_, ...), custom_call_target="tpu_custom_call" | custom-call | flops 3623878656 | bytes 1048576 | tf_op jit(solution)/shard_map/attend/pallas_call | solution.py:218
  68.7 4.9 %attend.9 = (bf16[128,896]{1,0:T(8,128)(2,1)S(1)}, bf16[128,896]{1,0:T(8,128)(2,1)S(1)}, bf16[128,896]{1,0:T(8,128)(2,1)S(1)}, bf16[128,896]{1,0:T(8,128)(2,1)S(1)}) custom-call(s32[4]{0:T(128)S(1)} %copy-done.5, f32[1,256]{1,0:T(1,128)S(1)} %bitcast.13, bf16[4,192,256]{2,1,0:T(8,128)(2,1)S(1)} %get-tuple-element.54.refs_2_, ...), custom_call_target="tpu_custom_call" | custom-call | flops 1811939328 | bytes 1048576 | tf_op jit(solution)/shard_map/attend/pallas_call | solution.py:218
  73.5 5.2 %collective-permute-start.17 = (bf16[128,896]{1,0:T(8,128)(2,1)S(1)}, bf16[128,896]{1,0:T(8,128)(2,1)S(1)}, u32[]{:S(2)}, u32[]{:S(2)}) collective-permute-start(bf16[128,896]{1,0:T(8,128)(2,1)S(1)} %get-tuple-element.83), channel_id=1, source_target_pairs={{0,0},{128,1},{1,64},{129,65},{64,128},{192,129},{65,192},{193,193... | collective-permute-start | bytes 688136 | tf_op jit(solution)/shard_map/ppermute | solution.py:369
  78.8 0.1 collective-permute-start.18
  78.9 1.0 %collective-permute-start.19 = (bf16[128,896]{1,0:T(8,128)(2,1)S(1)}, bf16[128,896]{1,0:T(8,128)(2,1)S(1)}, u32[]{:S(2)}, u32[]{:S(2)}) collective-permute-start(bf16[128,896]{1,0:T(8,128)(2,1)S(1)} %get-tuple-element.85), channel_id=1, source_target_pairs={{64,0},{192,1},{65,64},{193,65},{0,128},{128,129},{1,192},{129,193... | collective-permute-start | bytes 688136 | tf_op jit(solution)/shard_map/ppermute | solution.py:369
  79.9 4.4 %collective-permute-start.20 = (bf16[128,896]{1,0:T(8,128)(2,1)S(1)}, bf16[128,896]{1,0:T(8,128)(2,1)S(1)}, u32[]{:S(2)}, u32[]{:S(2)}) collective-permute-start(bf16[128,896]{1,0:T(8,128)(2,1)S(1)} %get-tuple-element.86), channel_id=1, source_target_pairs={{65,0},{193,1},{64,64},{192,65},{1,128},{129,129},{0,192},{128,193... | collective-permute-start | bytes 688136 | tf_op jit(solution)/shard_map/ppermute | solution.py:369
  84.3 0.5 collective-permute-done.17.refs_0_
  84.9 1.5 %collective-permute-done.18.refs_1_ = bf16[128,896]{1,0:T(8,128)(2,1)S(1)} collective-permute-done((bf16[128,896]{1,0:T(8,128)(2,1)S(1)}, bf16[128,896]{1,0:T(8,128)(2,1)S(1)}, u32[]{:S(2)}, u32[]{:S(2)}) %collective-permute-start.18) | collective-permute-done | bytes 229408 | tf_op jit(solution)/shard_map/ppermute | solution.py:369
  86.4 4.7 %collective-permute-done.19.refs_2_ = bf16[128,896]{1,0:T(8,128)(2,1)S(1)} collective-permute-done((bf16[128,896]{1,0:T(8,128)(2,1)S(1)}, bf16[128,896]{1,0:T(8,128)(2,1)S(1)}, u32[]{:S(2)}, u32[]{:S(2)}) %collective-permute-start.19) | collective-permute-done | bytes 229408 | tf_op jit(solution)/shard_map/ppermute | solution.py:369
  91.1 0.1 collective-permute-done.20.refs_3_
  91.2 1.3 %merge.1 = bf16[128,1536]{1,0:T(8,128)(2,1)} custom-call(bf16[128,896]{1,0:T(8,128)(2,1)S(1)} %collective-permute-done.17.refs_0_, bf16[128,896]{1,0:T(8,128)(2,1)S(1)} %collective-permute-done.18.refs_1_, bf16[128,896]{1,0:T(8,128)(2,1)S(1)} %collective-permute-done.19.refs_2_, bf16[128,896]{1,0:T(8,128)(2,1)S(1)} %collective-permute-done.20.refs_3_), custom_call_target="tpu_custom_call" | custom-call | tf_op jit(solution)/shard_map/merge/pallas_call | solution.py:253
  (43 shorter events, 0.8 us)
Async XLA Ops:
  0.0 35.3 %copy-start.5 = (s32[4]{0:T(128)S(1)}, s32[4]{0:T(128)}, u32[]{:S(2)}) copy-start(s32[4]{0:T(128)} %refs_0_.9) | copy-start | bytes 52
  0.8 15.0 %collective-permute-start.3 = (bf16[32,512]{1,0:T(8,128)(2,1)S(1)}, bf16[32,512]{1,0:T(8,128)(2,1)S(1)}, u32[]{:S(2)}, u32[]{:S(2)}) collective-permute-start(bf16[32,512]{1,0:T(8,128)(2,1)S(1)} %pad_maximum_fusion.2), channel_id=1, source_target_pairs={{0,2},{2,0},{1,3},{3,1},{4,6},{6,4},{5,7},{7,5},{8,10},{10,8},{9,1... | collective-permute-start | bytes 98312 | tf_op jit(solution)/shard_map/ppermute | solution.py:273
  8.5 7.3 %collective-permute-start = (bf16[128,1536]{1,0:T(8,128)(2,1)}, bf16[128,1536]{1,0:T(8,128)(2,1)S(1)}, u32[]{:S(2)}, u32[]{:S(2)}) collective-permute-start(bf16[128,1536]{1,0:T(8,128)(2,1)} %q_ref.1), channel_id=1, source_target_pairs={{0,1},{1,0},{2,3},{3,2},{4,5},{5,4},{6,7},{7,6},{8,9},{9,8},{10,11... | collective-permute-start | bytes 1179656 | tf_op jit(solution)/shard_map/ppermute | solution.py:273
  9.5 6.3 %collective-permute-start.1 = (bf16[128,256]{1,0:T(8,128)(2,1)}, bf16[128,256]{1,0:T(8,128)(2,1)S(1)}, u32[]{:S(2)}, u32[]{:S(2)}) collective-permute-start(bf16[128,256]{1,0:T(8,128)(2,1)} %k_ref.1), channel_id=1, source_target_pairs={{0,1},{1,0},{2,3},{3,2},{4,5},{5,4},{6,7},{7,6},{8,9},{9,8},{10,11... | collective-permute-start | bytes 196616 | tf_op jit(solution)/shard_map/ppermute | solution.py:273
  9.5 6.3 %collective-permute-start.2 = (bf16[128,256]{1,0:T(8,128)(2,1)}, bf16[128,256]{1,0:T(8,128)(2,1)S(1)}, u32[]{:S(2)}, u32[]{:S(2)}) collective-permute-start(bf16[128,256]{1,0:T(8,128)(2,1)} %v_ref.1), channel_id=1, source_target_pairs={{0,1},{1,0},{2,3},{3,2},{4,5},{5,4},{6,7},{7,6},{8,9},{9,8},{10,11... | collective-permute-start | bytes 196616 | tf_op jit(solution)/shard_map/ppermute | solution.py:273
  11.3 1.0 %copy-start = (bf16[128,1536]{1,0:T(8,128)(2,1)S(1)}, bf16[128,1536]{1,0:T(8,128)(2,1)}, u32[]{:S(2)}) copy-start(bf16[128,1536]{1,0:T(8,128)(2,1)} %q_ref.1) | copy-start | bytes 1179652
  12.3 0.8 copy-start.1
  13.1 0.8 copy-start.2
  13.9 0.8 copy-start.3
  14.7 0.8 copy-start.4
  15.9 6.8 %collective-permute-start.4 = (bf16[288,256]{1,0:T(8,128)(2,1)S(1)}, bf16[288,256]{1,0:T(8,128)(2,1)S(1)}, u32[]{:S(2)}, u32[]{:S(2)}) collective-permute-start(bf16[288,256]{1,0:T(8,128)(2,1)S(1)} %get-tuple-element.51), channel_id=1, source_target_pairs={{0,64},{64,128},{128,192},{192,0},{1,65},{65,129},{129,193},{193,1... | collective-permute-start | bytes 442376 | tf_op jit(solution)/shard_map/ppermute | solution.py:273
  17.2 9.6 %collective-permute-start.5 = (bf16[288,256]{1,0:T(8,128)(2,1)S(1)}, bf16[288,256]{1,0:T(8,128)(2,1)S(1)}, u32[]{:S(2)}, u32[]{:S(2)}) collective-permute-start(bf16[288,256]{1,0:T(8,128)(2,1)S(1)} %get-tuple-element.52), channel_id=1, source_target_pairs={{0,128},{64,192},{128,0},{192,64},{1,129},{65,193},{129,1},{193,65... | collective-permute-start | bytes 442376 | tf_op jit(solution)/shard_map/ppermute | solution.py:273
  19.6 7.2 %collective-permute-start.6 = (bf16[288,256]{1,0:T(8,128)(2,1)S(1)}, bf16[288,256]{1,0:T(8,128)(2,1)S(1)}, u32[]{:S(2)}, u32[]{:S(2)}) collective-permute-start(bf16[288,256]{1,0:T(8,128)(2,1)S(1)} %get-tuple-element.53), channel_id=1, source_target_pairs={{0,192},{64,0},{128,64},{192,128},{1,193},{65,1},{129,65},{193,129... | collective-permute-start | bytes 442376 | tf_op jit(solution)/shard_map/ppermute | solution.py:273
  26.9 8.5 %collective-permute-start.7 = (bf16[4,192,256]{2,1,0:T(8,128)(2,1)S(1)}, bf16[4,192,256]{2,1,0:T(8,128)(2,1)S(1)}, u32[]{:S(2)}, u32[]{:S(2)}) collective-permute-start(bf16[4,192,256]{2,1,0:T(8,128)(2,1)S(1)} %get-tuple-element.54.refs_2_), channel_id=1, source_target_pairs={{0,1},{1,0},{2,3},{3,2},{4,5},{5,4},{6,7},{7,6},{8,9},{9,8},{10,11... | collective-permute-start | bytes 1179656 | tf_op jit(solution)/shard_map/ppermute | solution.py:273
  27.8 6.0 %collective-permute-start.9 = (bf16[4,96,256]{2,1,0:T(8,128)(2,1)S(1)}, bf16[4,96,256]{2,1,0:T(8,128)(2,1)S(1)}, u32[]{:S(2)}, u32[]{:S(2)}) collective-permute-start(bf16[4,96,256]{2,1,0:T(8,128)(2,1)S(1)} %get-tuple-element.55), channel_id=1, source_target_pairs={{0,32},{1,5},{4,36},{5,9},{8,40},{9,13},{12,44},{13,1},{16,0},{17,... | collective-permute-start | bytes 589832 | tf_op jit(solution)/shard_map/ppermute | solution.py:299
  29.2 9.9 %collective-permute-start.8 = (bf16[4,96,256]{2,1,0:T(8,128)(2,1)S(1)}, bf16[4,96,256]{2,1,0:T(8,128)(2,1)S(1)}, u32[]{:S(2)}, u32[]{:S(2)}) collective-permute-start(bf16[4,96,256]{2,1,0:T(8,128)(2,1)S(1)} %get-tuple-element.55), channel_id=1, source_target_pairs={{0,16},{1,13},{4,20},{5,1},{8,24},{9,5},{12,28},{13,9},{16,48},{17... | collective-permute-start | bytes 589832 | tf_op jit(solution)/shard_map/ppermute | solution.py:299
  33.8 5.7 %collective-permute-start.10 = (bf16[4,96,256]{2,1,0:T(8,128)(2,1)S(1)}, bf16[4,96,256]{2,1,0:T(8,128)(2,1)S(1)}, u32[]{:S(2)}, u32[]{:S(2)}) collective-permute-start(bf16[4,96,256]{2,1,0:T(8,128)(2,1)S(1)} %collective-permute-done.9), channel_id=1, source_target_pairs={{0,32},{1,5},{4,36},{5,9},{8,40},{9,13},{12,44},{13,1},{16,0},{17,... | collective-permute-start | bytes 589832 | tf_op jit(solution)/shard_map/ppermute | solution.py:299
  34.1 9.0 %collective-permute-start.12 = (bf16[2,4,96,256]{3,2,1,0:T(8,128)(2,1)S(1)}, bf16[2,4,96,256]{3,2,1,0:T(8,128)(2,1)S(1)}, u32[]{:S(2)}, u32[]{:S(2)}) collective-permute-start(bf16[2,4,96,256]{3,2,1,0:T(8,128)(2,1)S(1)} %pad_maximum_fusion.refs_4_), channel_id=1, source_target_pairs={{0,4},{1,33},{4,8},{5,37},{8,12},{9,41},{12,0},{13,45},{16,20},{17... | collective-permute-start | bytes 1179656 | tf_op jit(solution)/shard_map/ppermute | solution.py:299
  39.6 11.7 %collective-permute-start.11 = (bf16[2,4,96,256]{3,2,1,0:T(8,128)(2,1)S(1)}, bf16[2,4,96,256]{3,2,1,0:T(8,128)(2,1)S(1)}, u32[]{:S(2)}, u32[]{:S(2)}) collective-permute-start(bf16[2,4,96,256]{3,2,1,0:T(8,128)(2,1)S(1)} %pad_maximum_fusion.1.refs_6_), channel_id=1, source_target_pairs={{0,4},{1,33},{4,8},{5,37},{8,12},{9,41},{12,0},{13,45},{16,20},{17... | collective-permute-start | bytes 1179656 | tf_op jit(solution)/shard_map/ppermute | solution.py:299
  43.1 8.4 %collective-permute-start.14 = (bf16[2,4,96,256]{3,2,1,0:T(8,128)(2,1)S(1)}, bf16[2,4,96,256]{3,2,1,0:T(8,128)(2,1)S(1)}, u32[]{:S(2)}, u32[]{:S(2)}) collective-permute-start(bf16[2,4,96,256]{3,2,1,0:T(8,128)(2,1)S(1)} %collective-permute-done.12.refs_7_), channel_id=1, source_target_pairs={{0,4},{1,33},{4,8},{5,37},{8,12},{9,41},{12,0},{13,45},{16,20},{17... | collective-permute-start | bytes 1179656 | tf_op jit(solution)/shard_map/ppermute | solution.py:299
  51.4 8.6 %collective-permute-start.13 = (bf16[2,4,96,256]{3,2,1,0:T(8,128)(2,1)S(1)}, bf16[2,4,96,256]{3,2,1,0:T(8,128)(2,1)S(1)}, u32[]{:S(2)}, u32[]{:S(2)}) collective-permute-start(bf16[2,4,96,256]{3,2,1,0:T(8,128)(2,1)S(1)} %collective-permute-done.11.refs_6_), channel_id=1, source_target_pairs={{0,4},{1,33},{4,8},{5,37},{8,12},{9,41},{12,0},{13,45},{16,20},{17... | collective-permute-start | bytes 1179656 | tf_op jit(solution)/shard_map/ppermute | solution.py:299
  51.5 11.1 %collective-permute-start.15 = (bf16[2,4,96,256]{3,2,1,0:T(8,128)(2,1)S(1)}, bf16[2,4,96,256]{3,2,1,0:T(8,128)(2,1)S(1)}, u32[]{:S(2)}, u32[]{:S(2)}) collective-permute-start(bf16[2,4,96,256]{3,2,1,0:T(8,128)(2,1)S(1)} %collective-permute-done.14.refs_7_), channel_id=1, source_target_pairs={{0,4},{1,33},{4,8},{5,37},{8,12},{9,41},{12,0},{13,45},{16,20},{17... | collective-permute-start | bytes 1179656 | tf_op jit(solution)/shard_map/ppermute | solution.py:299
  60.0 8.6 %collective-permute-start.16 = (bf16[2,4,96,256]{3,2,1,0:T(8,128)(2,1)S(1)}, bf16[2,4,96,256]{3,2,1,0:T(8,128)(2,1)S(1)}, u32[]{:S(2)}, u32[]{:S(2)}) collective-permute-start(bf16[2,4,96,256]{3,2,1,0:T(8,128)(2,1)S(1)} %collective-permute-done.13.refs_6_), channel_id=1, source_target_pairs={{0,4},{1,33},{4,8},{5,37},{8,12},{9,41},{12,0},{13,45},{16,20},{17... | collective-permute-start | bytes 1179656 | tf_op jit(solution)/shard_map/ppermute | solution.py:299
  73.5 11.3 %collective-permute-start.17 = (bf16[128,896]{1,0:T(8,128)(2,1)S(1)}, bf16[128,896]{1,0:T(8,128)(2,1)S(1)}, u32[]{:S(2)}, u32[]{:S(2)}) collective-permute-start(bf16[128,896]{1,0:T(8,128)(2,1)S(1)} %get-tuple-element.83), channel_id=1, source_target_pairs={{0,0},{128,1},{1,64},{129,65},{64,128},{192,129},{65,192},{193,193... | collective-permute-start | bytes 688136 | tf_op jit(solution)/shard_map/ppermute | solution.py:369
  78.8 7.6 %collective-permute-start.18 = (bf16[128,896]{1,0:T(8,128)(2,1)S(1)}, bf16[128,896]{1,0:T(8,128)(2,1)S(1)}, u32[]{:S(2)}, u32[]{:S(2)}) collective-permute-start(bf16[128,896]{1,0:T(8,128)(2,1)S(1)} %get-tuple-element.84), channel_id=1, source_target_pairs={{1,0},{129,1},{0,64},{128,65},{65,128},{193,129},{64,192},{192,193... | collective-permute-start | bytes 688136 | tf_op jit(solution)/shard_map/ppermute | solution.py:369
  78.9 12.2 %collective-permute-start.19 = (bf16[128,896]{1,0:T(8,128)(2,1)S(1)}, bf16[128,896]{1,0:T(8,128)(2,1)S(1)}, u32[]{:S(2)}, u32[]{:S(2)}) collective-permute-start(bf16[128,896]{1,0:T(8,128)(2,1)S(1)} %get-tuple-element.85), channel_id=1, source_target_pairs={{64,0},{192,1},{65,64},{193,65},{0,128},{128,129},{1,192},{129,193... | collective-permute-start | bytes 688136 | tf_op jit(solution)/shard_map/ppermute | solution.py:369
  79.9 11.3 %collective-permute-start.20 = (bf16[128,896]{1,0:T(8,128)(2,1)S(1)}, bf16[128,896]{1,0:T(8,128)(2,1)S(1)}, u32[]{:S(2)}, u32[]{:S(2)}) collective-permute-start(bf16[128,896]{1,0:T(8,128)(2,1)S(1)} %get-tuple-element.86), channel_id=1, source_target_pairs={{65,0},{193,1},{64,64},{192,65},{1,128},{129,129},{0,192},{128,193... | collective-permute-start | bytes 688136 | tf_op jit(solution)/shard_map/ppermute | solution.py:369

commit v2 on v1

--- a/solution.py
+++ b/solution.py
@@ -47,8 +47,9 @@
         out[BLOCK + i * HALF : BLOCK + (i + 1) * HALF, :] = q[rows, lanes]
 
 
-def deal_body(q_ref, k_ref, v_ref, ck_ref, cv_ref, *outs):
-    x, half, core = lax.axis_index("x"), lax.axis_index("zh"), lax.axis_index("core")
+def deal_body(q_ref, kv_ref, c_ref, *outs):
+    x, core = lax.axis_index("x"), lax.axis_index("core")
+    k_ref, v_ref = kv_ref.at[:, : 2 * D], kv_ref.at[:, 2 * D :]
     for s in range(4):
         head, out = (x + s) & 3, outs[s]
 
@@ -56,9 +57,9 @@
         def _(head=head, out=out):
             from_one_core(head, q_ref, k_ref, v_ref, out)
 
-        lanes = aligned(half * 4 + head, D)
-        out[HALF : HALF + 16, :D] = ck_ref[:, lanes]
-        out[HALF : HALF + 16, D:] = cv_ref[:, lanes]
+        lanes = aligned(head, D)
+        out[HALF : HALF + 16, :D] = c_ref[:16, lanes]
+        out[HALF : HALF + 16, D:] = c_ref[16:, lanes]
 
 
 def deal(*own):
@@ -128,11 +129,12 @@
     q_refs, refs = refs[:2], refs[2:]
     if not first:
         acc, top, *refs = refs
-    q_all, keys, vals, *made = refs[-4:] if last else refs[-3:]
-    blocks, outs = (refs[:-8], refs[-8:-4]) if last else (refs[:-5], refs[-5:-3])
+    ending = last is not None
+    q_all, keys, vals = refs[-3:]
+    blocks, outs = (refs[:-4], refs[-4:-3]) if ending else (refs[:-5], refs[-5:-3])
     blocks = [pair.at[i] for pair in blocks for i in range(2)]
     total = keys.shape[0]
-    for h in range(2):
+    for h in [last] if ending else range(2):
         for c in range(4):
             for g in range(GROUP):
                 rows = slice(g // 2 * HALF, (g // 2 + 1) * HALF)
@@ -148,7 +150,6 @@
             at += depth
     vals[:, D:] = jnp.ones((total, D), BF)
     paged = 4 * CROWS * len(blocks)
-    core = lax.axis_index("core")
     lane = lax.broadcasted_iota(jnp.int32, (HALF, D), 1)
 
     def seen(c):
@@ -174,24 +175,23 @@
         if not first:
             factor = jnp.exp2((old - new) * SCALE)
             out, norm = acc[h, c, :, :D] * factor + out, acc[h, c, :, D:] * factor + norm
-        if not last:
+        if not ending:
             outs[0][h, c, :, :D] = out
             outs[0][h, c, :, D:] = norm
             outs[1][h, c] = new
             return
         out = (out / norm).astype(BF)
         log = new * SCALE + jnp.log2(norm)
-        rows = aligned((core + h) & 1, HALF)
         logs = jnp.zeros((HALF, D), F32)
         for g in range(GROUP):
             part = slice(g * HALF, (g + 1) * HALF)
-            made[0][c, rows, g * D : (g + 1) * D] = out[part, :]
+            outs[0][c, :, g * D : (g + 1) * D] = out[part, :]
             left = log[part, :]
             for i in range(3):
                 term = left.astype(BF).astype(F32)
                 logs = jnp.where(lane == 3 * g + i, term, logs)
                 left = left - term
-        made[0][c, rows, WIDE:] = logs.astype(BF)
+        outs[0][c, :, WIDE:] = logs.astype(BF)
 
     def token_half(h, carry):
         ahead = scores(h, 3)
@@ -200,19 +200,18 @@
             absorb(h, c, now)
         return carry
 
-    lax.fori_loop(0, 2, token_half, 0)
-    if last:
-        r = slot()
-        for s in range(4):
-            outs[s][...] = made[0][r ^ s]
-
-
-def attend(q, state, pairs, window, bias, last=False):
+    if ending:
+        token_half(last, 0)
+    else:
+        lax.fori_loop(0, 2, token_half, 0)
+
+
+def attend(q, state, pairs, window, bias, last=None):
     total = BLOCK * 8 * len(pairs)
     kept = [] if state is None else list(state)
     work = 16 * ROWS * len(pairs) * (4 * CROWS + 2.5 * HALF)
-    if last:
-        shapes = [shaped((2 * HALF, WIDE + D))] * 4
+    if last is not None:
+        shapes = [shaped((4, HALF, WIDE + D))]
     else:
         shapes = [shaped((2, 4, ROWS, 2 * D), F32), shaped((2, 4, ROWS, D), F32)]
     return pl.pallas_call(
@@ -224,8 +223,7 @@
             VMEM((2, 4, ROWS, D), BF),
             VMEM((total, D), BF),
             VMEM((total, 2 * D), BF),
-        ]
-        + ([VMEM((4, 2 * HALF, WIDE + D), BF)] if last else []),
+        ],
         compiler_params=pltpu.CompilerParams(vmem_limit_bytes=40 * 2**20),
         cost_estimate=pl.CostEstimate(
             flops=int(work * D * 4 * 2), bytes_accessed=2**20, transcendentals=int(work)
@@ -234,30 +232,47 @@
     )(window, bias, *q, *kept, *pairs)
 
 
-def merge_body(*refs):
-    out = refs[4]
-    x = lax.axis_index("x")
+def merge_body(one, two, *outs):
+    r = slot()
     lane = lax.broadcasted_iota(jnp.int32, (D, WIDE), 0)
     head = lax.broadcasted_iota(jnp.int32, (D, WIDE), 1) // D
     pick = jnp.where((lane // 3 == head) & (lane < 3 * GROUP), 1.0, 0.0).astype(BF)
-    for pair in range(2):
-        one, two = refs[2 * pair], refs[2 * pair + 1]
-        a, b = (jnp.dot(ref[:, WIDE:], pick, preferred_element_type=F32) for ref in (one, two))
+    for s in range(4):
+        refs = one[r ^ s], two[r ^ s]
+        a, b = (jnp.dot(ref[:, WIDE:], pick, preferred_element_type=F32) for ref in refs)
         most = jnp.maximum(a, b)
         a, b = jnp.exp2(a - most), jnp.exp2(b - most)
-        both = (one[:, :WIDE].astype(F32) * a + two[:, :WIDE].astype(F32) * b) / (a + b)
-        out[:, aligned((x >> 1) ^ pair, WIDE)] = both.astype(BF)
-
-
-def merge(messages):
+        both = (refs[0][:, :WIDE].astype(F32) * a + refs[1][:, :WIDE].astype(F32) * b) / (a + b)
+        outs[s][...] = both.astype(BF)
+
+
+def merge(one, two):
     return pl.pallas_call(
         merge_body,
+        in_specs=[vmem] * 2,
+        out_specs=[vmem] * 4,
+        out_shape=[shaped((HALF, WIDE))] * 4,
+        compiler_params=small,
+        name="merge",
+    )(one, two)
+
+
+def place_body(*refs):
+    x = lax.axis_index("x")
+    for s in range(4):
+        piece = x ^ s
+        refs[4][aligned(piece & 1, HALF), aligned(piece >> 1, WIDE)] = refs[s][...]
+
+
+def place(pieces):
+    return pl.pallas_call(
+        place_body,
         in_specs=[vmem] * 4,
         out_specs=vmem,
         out_shape=shaped((2 * HALF, 2 * WIDE)),
         compiler_params=small,
-        name="merge",
-    )(*messages)
+        name="place",
+    )(*pieces)
 
 
 def spread(s):
@@ -336,10 +351,15 @@
 
 def on_device(queries, keys, values, cache_keys, cache_values, page_owner, window):
     got = [swap(one) for one in (queries, keys, values)]
-    start = 4 * D * (1 - lax.axis_index("zh"))
-    halves = [lax.dynamic_slice_in_dim(c, start, 4 * D, 1) for c in (cache_keys, cache_values)]
-    got.append(shift(jnp.concatenate(halves), "zh", 1, 2))
-    messages = fill(got, deal(queries, keys, values, cache_keys, cache_values))
+    half = lax.axis_index("zh")
+    own, other = (
+        jnp.concatenate(
+            [lax.dynamic_slice_in_dim(c, 4 * D * h, 4 * D, 1) for c in (cache_keys, cache_values)]
+        )
+        for h in (half, 1 - half)
+    )
+    got.append(shift(other, "zh", 1, 2))
+    messages = fill(got, deal(queries, jnp.concatenate([keys, values], axis=1), own))
     messages = [messages[0]] + [shift(messages[s], "x", s) for s in range(1, 4)]
     block, mine = join(messages)
     q = [mine, swap(mine)]
@@ -357,18 +377,19 @@
             if state is not None:
                 before, *state = lax.optimization_barrier((before, *state))
             pairs[pair, b] = step_on(before, 1)
-        state = attend(
-            q,
-            state,
-            [pairs[one] for one in piece],
-            window,
-            cache_bias(page_owner, [(a, b) for pair, b in piece for a in PAIRS[pair]]),
-            last=piece is PIECES[-1],
-        )
+        parts = [pairs[one] for one in piece]
+        bias = cache_bias(page_owner, [(a, b) for pair, b in piece for a in PAIRS[pair]])
+        if piece is not PIECES[-1]:
+            state = attend(q, state, parts, window, bias)
+    (theirs,) = attend(q, state, parts, window, bias, last=1)
+    theirs, *state = lax.optimization_barrier((theirs, *state))
+    theirs = swap(theirs)
+    (mine,) = attend(q, state, parts, window, bias, last=0)
+    pieces = merge(mine, theirs)
     back = [
-        lax.ppermute(state[s], ("x", "core"), [(b, a) for a, b in spread(s)]) for s in range(4)
+        lax.ppermute(pieces[s], ("x", "core"), [(b, a) for a, b in spread(s)]) for s in range(4)
     ]
-    return merge(back)
+    return place(back)
 
 
 def solution(mesh):

time: 92.9 us -> 87.7 us (0.944)
  waiting for transfers between devices: 19.9 us -> 16.3 us
  local copies, waits for them, and re-layouts: 6.08 us -> 2.93 us
    ppermute x4, waiting for transfers between devices: 6.85 us -> 3.22 us  [on_device(): lax.ppermute(pieces[s], ('x', 'core'), [(b, a) for a, b in spread(s)])]
    unnamed x12 -> x4, local copies, waits for them, and re-layouts: 4.19 us -> 1 us
    ppermute x8 -> x9, starting transfers between devices: 15 us -> 17.5 us  [shift(): lax.ppermute(array, axis, [(i, (i + by) % size) for i in range(size)])]
    ppermute x4, starting transfers between devices: 10.8 us -> 8.35 us  [on_device(): lax.ppermute(pieces[s], ('x', 'core'), [(b, a) for a, b in spread(s)])]
    pallas_call x5 -> x6, Pallas kernels: 26.8 us -> 27.3 us  [attend(): pl.pallas_call(lambda *refs: attend_body(state is None, last, refs), in_s...]
    ppermute x8 -> x9, waiting for transfers between devices: 6.02 us -> 6.04 us  [shift(): lax.ppermute(array, axis, [(i, (i + by) % size) for i in range(size)])]
  transfers between devices with their start and end apart: 21 -> 22, of which waited for: 10 -> 9; matrix products, arithmetic and copies ran while one was open for 2% -> 3% of each run, Pallas kernels for 24% -> 28%
where the time goes in v2:
time: 87.7 us; the launch traced here: 87.3 us
  starting transfers between devices  37.5 us (43%)
  Pallas kernels  28.8 us (33%)
  waiting for transfers between devices  16.3 us (19%)
  local copies, waits for them, and re-layouts  2.93 us (3%)
  other arithmetic  1.41 us (2%)
    pallas_call x6, Pallas kernels, attend(): pl.pallas_call(lambda *refs: attend_body(state is None, last, refs), in_s...  27.3 us
    ppermute x9, starting transfers between devices, shift(): lax.ppermute(array, axis, [(i, (i + by) % size) for i in range(size)])  17.5 us
    ppermute x9, starting transfers between devices, step_on(): return lax.ppermute(block, ('zl', 'y', 'core'), pairs)  11.6 us
    ppermute x4, starting transfers between devices, on_device(): lax.ppermute(pieces[s], ('x', 'core'), [(b, a) for a, b in spread(s)])  8.35 us
    ppermute x9, waiting for transfers between devices, step_on(): return lax.ppermute(block, ('zl', 'y', 'core'), pairs)  7.07 us
    ppermute x9, waiting for transfers between devices, shift(): lax.ppermute(array, axis, [(i, (i + by) % size) for i in range(size)])  6.04 us
    ppermute x4, waiting for transfers between devices, on_device(): lax.ppermute(pieces[s], ('x', 'core'), [(b, a) for a, b in spread(s)])  3.22 us
  transfers between devices with their start and end apart: 22, of which 9 were waited for; matrix products, arithmetic and copies ran while one was open for 3% of the time, Pallas kernels for 28%

profile of v2, /device:TPU:1, one launch (start us, length us, event | category | flops | bytes accessed | tf_op | source)
XLA Modules:
  0.0 87.3 jit_solution(5322354842529589980)
XLA Ops:
  0.0 0.8 constant_dynamic-slice_fusion
  0.8 7.8 %collective-permute-start.3 = (bf16[32,512]{1,0:T(8,128)(2,1)S(1)}, bf16[32,512]{1,0:T(8,128)(2,1)S(1)}, u32[]{:S(2)}, u32[]{:S(2)}) collective-permute-start(bf16[32,512]{1,0:T(8,128)(2,1)S(1)} %pad_maximum_fusion.3), channel_id=1, source_target_pairs={{0,2},{2,0},{1,3},{3,1},{4,6},{6,4},{5,7},{7,5},{8,10},{10,8},{9,1... | collective-permute-start | bytes 98312 | tf_op jit(solution)/shard_map/ppermute | solution.py:288
  8.6 1.0 %collective-permute-start = (bf16[128,1536]{1,0:T(8,128)(2,1)}, bf16[128,1536]{1,0:T(8,128)(2,1)S(1)}, u32[]{:S(2)}, u32[]{:S(2)}) collective-permute-start(bf16[128,1536]{1,0:T(8,128)(2,1)} %q_ref.1), channel_id=1, source_target_pairs={{0,1},{1,0},{2,3},{3,2},{4,5},{5,4},{6,7},{7,6},{8,9},{9,8},{10,11... | collective-permute-start | bytes 1179656 | tf_op jit(solution)/shard_map/ppermute | solution.py:288
  9.6 0.5 collective-permute-start.2
  10.1 0.9 %pad_maximum_fusion.2.kv_ref = bf16[128,512]{1,0:T(8,128)(2,1)S(1)} fusion(bf16[128,256]{1,0:T(8,128)(2,1)} %param.9, bf16[128,256]{1,0:T(8,128)(2,1)} %param.8), kind=kLoop, calls=%fused_computation.2 | loop fusion | flops 262144 | bytes 262144 | tf_op jit(solution)/shard_map/concatenate | solution.py:362
  11.1 0.7 slice.2
  11.8 0.1 multiply_add_fusion.1
  11.9 0.1 reshape.768
  12.1 0.1 reshape.770
  12.2 0.1 compare_reduce_fusion
  12.4 0.1 reshape.757
  12.6 1.0 %copy-done = bf16[128,1536]{1,0:T(8,128)(2,1)S(1)} copy-done((bf16[128,1536]{1,0:T(8,128)(2,1)S(1)}, bf16[128,1536]{1,0:T(8,128)(2,1)}, u32[]{:S(2)}) %copy-start) | copy-done | bytes 393240
  13.6 0.1 fill.1
  13.8 1.3 %collective-permute-start.4 = (bf16[288,256]{1,0:T(8,128)(2,1)S(1)}, bf16[288,256]{1,0:T(8,128)(2,1)S(1)}, u32[]{:S(2)}, u32[]{:S(2)}) collective-permute-start(bf16[288,256]{1,0:T(8,128)(2,1)S(1)} %get-tuple-element.54), channel_id=1, source_target_pairs={{0,64},{64,128},{128,192},{192,0},{1,65},{65,129},{129,193},{193,1... | collective-permute-start | bytes 442376 | tf_op jit(solution)/shard_map/ppermute | solution.py:288
  15.1 2.5 %collective-permute-start.5 = (bf16[288,256]{1,0:T(8,128)(2,1)S(1)}, bf16[288,256]{1,0:T(8,128)(2,1)S(1)}, u32[]{:S(2)}, u32[]{:S(2)}) collective-permute-start(bf16[288,256]{1,0:T(8,128)(2,1)S(1)} %get-tuple-element.55), channel_id=1, source_target_pairs={{0,128},{64,192},{128,0},{192,64},{1,129},{65,193},{129,1},{193,65... | collective-permute-start | bytes 442376 | tf_op jit(solution)/shard_map/ppermute | solution.py:288
  17.5 1.2 %collective-permute-start.6 = (bf16[288,256]{1,0:T(8,128)(2,1)S(1)}, bf16[288,256]{1,0:T(8,128)(2,1)S(1)}, u32[]{:S(2)}, u32[]{:S(2)}) collective-permute-start(bf16[288,256]{1,0:T(8,128)(2,1)S(1)} %get-tuple-element.56), channel_id=1, source_target_pairs={{0,192},{64,0},{128,64},{192,128},{1,193},{65,1},{129,65},{193,129... | collective-permute-start | bytes 442376 | tf_op jit(solution)/shard_map/ppermute | solution.py:288
  18.7 1.8 %collective-permute-done.4.refs_1_ = bf16[288,256]{1,0:T(8,128)(2,1)S(1)} collective-permute-done((bf16[288,256]{1,0:T(8,128)(2,1)S(1)}, bf16[288,256]{1,0:T(8,128)(2,1)S(1)}, u32[]{:S(2)}, u32[]{:S(2)}) %collective-permute-start.4) | collective-permute-done | bytes 147488 | tf_op jit(solution)/shard_map/ppermute | solution.py:288
  20.5 4.2 %collective-permute-done.5.refs_2_ = bf16[288,256]{1,0:T(8,128)(2,1)S(1)} collective-permute-done((bf16[288,256]{1,0:T(8,128)(2,1)S(1)}, bf16[288,256]{1,0:T(8,128)(2,1)S(1)}, u32[]{:S(2)}, u32[]{:S(2)}) %collective-permute-start.5) | collective-permute-done | bytes 147488 | tf_op jit(solution)/shard_map/ppermute | solution.py:288
  24.7 0.9 collective-permute-start.7
  25.6 0.1 compare_reduce_fusion.3
  25.7 1.4 %collective-permute-start.9 = (bf16[4,96,256]{2,1,0:T(8,128)(2,1)S(1)}, bf16[4,96,256]{2,1,0:T(8,128)(2,1)S(1)}, u32[]{:S(2)}, u32[]{:S(2)}) collective-permute-start(bf16[4,96,256]{2,1,0:T(8,128)(2,1)S(1)} %get-tuple-element.58), channel_id=1, source_target_pairs={{0,32},{1,5},{4,36},{5,9},{8,40},{9,13},{12,44},{13,1},{16,0},{17,... | collective-permute-start | bytes 589832 | tf_op jit(solution)/shard_map/ppermute | solution.py:314
  27.1 1.5 %collective-permute-start.8 = (bf16[4,96,256]{2,1,0:T(8,128)(2,1)S(1)}, bf16[4,96,256]{2,1,0:T(8,128)(2,1)S(1)}, u32[]{:S(2)}, u32[]{:S(2)}) collective-permute-start(bf16[4,96,256]{2,1,0:T(8,128)(2,1)S(1)} %get-tuple-element.58), channel_id=1, source_target_pairs={{0,16},{1,13},{4,20},{5,1},{8,24},{9,5},{12,28},{13,9},{16,48},{17... | collective-permute-start | bytes 589832 | tf_op jit(solution)/shard_map/ppermute | solution.py:314
  28.6 3.1 %collective-permute-done.9 = bf16[4,96,256]{2,1,0:T(8,128)(2,1)S(1)} collective-permute-done((bf16[4,96,256]{2,1,0:T(8,128)(2,1)S(1)}, bf16[4,96,256]{2,1,0:T(8,128)(2,1)S(1)}, u32[]{:S(2)}, u32[]{:S(2)}) %collective-permute-start.9) | collective-permute-done | bytes 196640 | tf_op jit(solution)/shard_map/ppermute | solution.py:314
  31.7 0.2 collective-permute-start.10
  31.9 1.3 %collective-permute-start.12 = (bf16[2,4,96,256]{3,2,1,0:T(8,128)(2,1)S(1)}, bf16[2,4,96,256]{3,2,1,0:T(8,128)(2,1)S(1)}, u32[]{:S(2)}, u32[]{:S(2)}) collective-permute-start(bf16[2,4,96,256]{3,2,1,0:T(8,128)(2,1)S(1)} %pad_maximum_fusion.refs_4_), channel_id=1, source_target_pairs={{0,4},{1,33},{4,8},{5,37},{8,12},{9,41},{12,0},{13,45},{16,20},{17... | collective-permute-start | bytes 1179656 | tf_op jit(solution)/shard_map/ppermute | solution.py:314
  33.2 3.7 %attend.6 = (f32[2,4,384,256]{3,2,1,0:T(8,128)S(1)}, f32[2,4,384,128]{3,2,1,0:T(8,128)S(1)}) custom-call(s32[4]{0:T(128)S(1)} %copy-done.1, f32[1,256]{1,0:T(1,128)S(1)} %bitcast.15, bf16[4,192,256]{2,1,0:T(8,128)(2,1)S(1)} %get-tuple-element.57.refs_2_, bf16[4,192,256]{2,1,0:T(8,128)(2,1)S(1)} %collective-permute-done.7.refs_3_, ...), custom_call_target="tpu_custom_call" | custom-call | flops 1811939328 | bytes 1048576 | tf_op jit(solution)/shard_map/attend/pallas_call | solution.py:217
  37.0 0.5 collective-permute-done.10
  37.5 2.3 %collective-permute-start.11 = (bf16[2,4,96,256]{3,2,1,0:T(8,128)(2,1)S(1)}, bf16[2,4,96,256]{3,2,1,0:T(8,128)(2,1)S(1)}, u32[]{:S(2)}, u32[]{:S(2)}) collective-permute-start(bf16[2,4,96,256]{3,2,1,0:T(8,128)(2,1)S(1)} %pad_maximum_fusion.1.refs_6_), channel_id=1, source_target_pairs={{0,4},{1,33},{4,8},{5,37},{8,12},{9,41},{12,0},{13,45},{16,20},{17... | collective-permute-start | bytes 1179656 | tf_op jit(solution)/shard_map/ppermute | solution.py:314
  39.8 1.2 %collective-permute-done.12.refs_7_ = bf16[2,4,96,256]{3,2,1,0:T(8,128)(2,1)S(1)} collective-permute-done((bf16[2,4,96,256]{3,2,1,0:T(8,128)(2,1)S(1)}, bf16[2,4,96,256]{3,2,1,0:T(8,128)(2,1)S(1)}, u32[]{:S(2)}, u32[]{:S(2)}) %collective-permute-start.12) | collective-permute-done | bytes 393248 | tf_op jit(solution)/shard_map/ppermute | solution.py:314
  41.0 2.2 %collective-permute-start.14 = (bf16[2,4,96,256]{3,2,1,0:T(8,128)(2,1)S(1)}, bf16[2,4,96,256]{3,2,1,0:T(8,128)(2,1)S(1)}, u32[]{:S(2)}, u32[]{:S(2)}) collective-permute-start(bf16[2,4,96,256]{3,2,1,0:T(8,128)(2,1)S(1)} %collective-permute-done.12.refs_7_), channel_id=1, source_target_pairs={{0,4},{1,33},{4,8},{5,37},{8,12},{9,41},{12,0},{13,45},{16,20},{17... | collective-permute-start | bytes 1179656 | tf_op jit(solution)/shard_map/ppermute | solution.py:314
  43.1 6.1 %attend.7 = (f32[2,4,384,256]{3,2,1,0:T(8,128)S(1)}, f32[2,4,384,128]{3,2,1,0:T(8,128)S(1)}) custom-call(s32[4]{0:T(128)S(1)} %copy-done.1, f32[1,512]{1,0:T(1,128)S(1)} %bitcast.10, bf16[4,192,256]{2,1,0:T(8,128)(2,1)S(1)} %get-tuple-element.57.refs_2_, bf16[4,192,256]{2,1,0:T(8,128)(2,1)S(1)} %collective-permute-done.7.refs_3_, ...), custom_call_target="tpu_custom_call" | custom-call | flops 3623878656 | bytes 1048576 | tf_op jit(solution)/shard_map/attend/pallas_call | solution.py:217
  49.4 2.4 %collective-permute-start.15 = (bf16[2,4,96,256]{3,2,1,0:T(8,128)(2,1)S(1)}, bf16[2,4,96,256]{3,2,1,0:T(8,128)(2,1)S(1)}, u32[]{:S(2)}, u32[]{:S(2)}) collective-permute-start(bf16[2,4,96,256]{3,2,1,0:T(8,128)(2,1)S(1)} %collective-permute-done.14.refs_7_), channel_id=1, source_target_pairs={{0,4},{1,33},{4,8},{5,37},{8,12},{9,41},{12,0},{13,45},{16,20},{17... | collective-permute-start | bytes 1179656 | tf_op jit(solution)/shard_map/ppermute | solution.py:314
  51.8 6.1 %attend.8 = (f32[2,4,384,256]{3,2,1,0:T(8,128)S(1)}, f32[2,4,384,128]{3,2,1,0:T(8,128)S(1)}) custom-call(s32[4]{0:T(128)S(1)} %copy-done.1, f32[1,512]{1,0:T(1,128)S(1)} %bitcast.11, bf16[4,192,256]{2,1,0:T(8,128)(2,1)S(1)} %get-tuple-element.57.refs_2_, bf16[4,192,256]{2,1,0:T(8,128)(2,1)S(1)} %collective-permute-done.7.refs_3_, ...), custom_call_target="tpu_custom_call" | custom-call | flops 3623878656 | bytes 1048576 | tf_op jit(solution)/shard_map/attend/pallas_call | solution.py:217
  57.9 0.3 collective-permute-start.16
  58.2 2.2 %collective-permute-done.15.refs_7_ = bf16[2,4,96,256]{3,2,1,0:T(8,128)(2,1)S(1)} collective-permute-done((bf16[2,4,96,256]{3,2,1,0:T(8,128)(2,1)S(1)}, bf16[2,4,96,256]{3,2,1,0:T(8,128)(2,1)S(1)}, u32[]{:S(2)}, u32[]{:S(2)}) %collective-permute-start.15) | collective-permute-done | bytes 393248 | tf_op jit(solution)/shard_map/ppermute | solution.py:314
  60.4 6.1 %attend.9 = (f32[2,4,384,256]{3,2,1,0:T(8,128)S(1)}, f32[2,4,384,128]{3,2,1,0:T(8,128)S(1)}) custom-call(s32[4]{0:T(128)S(1)} %copy-done.1, f32[1,512]{1,0:T(1,128)S(1)} %bitcast.12, bf16[4,192,256]{2,1,0:T(8,128)(2,1)S(1)} %get-tuple-element.57.refs_2_, bf16[4,192,256]{2,1,0:T(8,128)(2,1)S(1)} %collective-permute-done.7.refs_3_, ...), custom_call_target="tpu_custom_call" | custom-call | flops 3623878656 | bytes 1048576 | tf_op jit(solution)/shard_map/attend/pallas_call | solution.py:217
  66.5 2.7 %attend.10 = bf16[4,64,896]{2,1,0:T(8,128)(2,1)S(1)} custom-call(s32[4]{0:T(128)S(1)} %copy-done.1, f32[1,256]{1,0:T(1,128)S(1)} %bitcast.13, bf16[4,192,256]{2,1,0:T(8,128)(2,1)S(1)} %get-tuple-element.57.refs_2_, bf16[4,192,256]{2,1,0:T(8,128)(2,1)S(1)} %collective-permute-done.7.refs_3_, f32[2,4,384,256]{3,2,1,0:T(8,128)S(1)} %get-tuple-element.86.refs_4_, ...), custom_call_target="tpu_custom_call" | custom-call | flops 1811939328 | bytes 1048576 | tf_op jit(solution)/shard_map/attend/pallas_call | solution.py:217
  69.2 2.5 %collective-permute-start.17 = (bf16[4,64,896]{2,1,0:T(8,128)(2,1)S(1)}, bf16[4,64,896]{2,1,0:T(8,128)(2,1)S(1)}, u32[]{:S(2)}, u32[]{:S(2)}) collective-permute-start(bf16[4,64,896]{2,1,0:T(8,128)(2,1)S(1)} %attend.10), channel_id=1, source_target_pairs={{0,1},{1,0},{2,3},{3,2},{4,5},{5,4},{6,7},{7,6},{8,9},{9,8},{10,11... | collective-permute-start | bytes 1376264 | tf_op jit(solution)/shard_map/ppermute | solution.py:288
  71.7 2.7 %attend.11.one = bf16[4,64,896]{2,1,0:T(8,128)(2,1)S(1)} custom-call(s32[4]{0:T(128)S(1)} %copy-done.1, f32[1,256]{1,0:T(1,128)S(1)} %bitcast.14, bf16[4,192,256]{2,1,0:T(8,128)(2,1)S(1)} %get-tuple-element.57.refs_2_, bf16[4,192,256]{2,1,0:T(8,128)(2,1)S(1)} %collective-permute-done.7.refs_3_, f32[2,4,384,256]{3,2,1,0:T(8,128)S(1)} %get-tuple-element.86.refs_4_, ...), custom_call_target="tpu_custom_call" | custom-call | flops 1811939328 | bytes 1048576 | tf_op jit(solution)/shard_map/attend/pallas_call | solution.py:217
  74.4 0.5 merge.1
  74.9 2.8 %collective-permute-start.18 = (bf16[64,768]{1,0:T(8,128)(2,1)S(1)}, bf16[64,768]{1,0:T(8,128)(2,1)S(1)}, u32[]{:S(2)}, u32[]{:S(2)}) collective-permute-start(bf16[64,768]{1,0:T(8,128)(2,1)S(1)} %get-tuple-element.89), channel_id=1, source_target_pairs={{0,0},{128,1},{1,64},{129,65},{64,128},{192,129},{65,192},{193,193... | collective-permute-start | bytes 294920 | tf_op jit(solution)/shard_map/ppermute | solution.py:390
  77.8 0.1 collective-permute-start.19
  77.8 2.1 %collective-permute-start.20 = (bf16[64,768]{1,0:T(8,128)(2,1)S(1)}, bf16[64,768]{1,0:T(8,128)(2,1)S(1)}, u32[]{:S(2)}, u32[]{:S(2)}) collective-permute-start(bf16[64,768]{1,0:T(8,128)(2,1)S(1)} %get-tuple-element.91), channel_id=1, source_target_pairs={{64,0},{192,1},{65,64},{193,65},{0,128},{128,129},{1,192},{129,193... | collective-permute-start | bytes 294920 | tf_op jit(solution)/shard_map/ppermute | solution.py:390
  80.0 3.3 %collective-permute-start.21 = (bf16[64,768]{1,0:T(8,128)(2,1)S(1)}, bf16[64,768]{1,0:T(8,128)(2,1)S(1)}, u32[]{:S(2)}, u32[]{:S(2)}) collective-permute-start(bf16[64,768]{1,0:T(8,128)(2,1)S(1)} %get-tuple-element.92), channel_id=1, source_target_pairs={{65,0},{193,1},{64,64},{192,65},{1,128},{129,129},{0,192},{128,193... | collective-permute-start | bytes 294920 | tf_op jit(solution)/shard_map/ppermute | solution.py:390
  83.3 0.2 collective-permute-done.19.refs_1_
  83.5 0.9 %collective-permute-done.20.refs_2_ = bf16[64,768]{1,0:T(8,128)(2,1)S(1)} collective-permute-done((bf16[64,768]{1,0:T(8,128)(2,1)S(1)}, bf16[64,768]{1,0:T(8,128)(2,1)S(1)}, u32[]{:S(2)}, u32[]{:S(2)}) %collective-permute-start.20) | collective-permute-done | bytes 98336 | tf_op jit(solution)/shard_map/ppermute | solution.py:390
  84.5 2.1 %collective-permute-done.21.refs_3_ = bf16[64,768]{1,0:T(8,128)(2,1)S(1)} collective-permute-done((bf16[64,768]{1,0:T(8,128)(2,1)S(1)}, bf16[64,768]{1,0:T(8,128)(2,1)S(1)}, u32[]{:S(2)}, u32[]{:S(2)}) %collective-permute-start.21) | collective-permute-done | bytes 98336 | tf_op jit(solution)/shard_map/ppermute | solution.py:390
  86.5 0.8 place.1
  (41 shorter events, 0.7 us)
Async XLA Ops:
  0.0 33.2 %copy-start.1 = (s32[4]{0:T(128)S(1)}, s32[4]{0:T(128)}, u32[]{:S(2)}) copy-start(s32[4]{0:T(128)} %refs_0_.11) | copy-start | bytes 52
  0.8 12.8 %collective-permute-start.3 = (bf16[32,512]{1,0:T(8,128)(2,1)S(1)}, bf16[32,512]{1,0:T(8,128)(2,1)S(1)}, u32[]{:S(2)}, u32[]{:S(2)}) collective-permute-start(bf16[32,512]{1,0:T(8,128)(2,1)S(1)} %pad_maximum_fusion.3), channel_id=1, source_target_pairs={{0,2},{2,0},{1,3},{3,1},{4,6},{6,4},{5,7},{7,5},{8,10},{10,8},{9,1... | collective-permute-start | bytes 98312 | tf_op jit(solution)/shard_map/ppermute | solution.py:288
  8.6 5.0 %collective-permute-start = (bf16[128,1536]{1,0:T(8,128)(2,1)}, bf16[128,1536]{1,0:T(8,128)(2,1)S(1)}, u32[]{:S(2)}, u32[]{:S(2)}) collective-permute-start(bf16[128,1536]{1,0:T(8,128)(2,1)} %q_ref.1), channel_id=1, source_target_pairs={{0,1},{1,0},{2,3},{3,2},{4,5},{5,4},{6,7},{7,6},{8,9},{9,8},{10,11... | collective-permute-start | bytes 1179656 | tf_op jit(solution)/shard_map/ppermute | solution.py:288
  9.6 4.0 %collective-permute-start.1 = (bf16[128,256]{1,0:T(8,128)(2,1)}, bf16[128,256]{1,0:T(8,128)(2,1)S(1)}, u32[]{:S(2)}, u32[]{:S(2)}) collective-permute-start(bf16[128,256]{1,0:T(8,128)(2,1)} %param.8), channel_id=1, source_target_pairs={{0,1},{1,0},{2,3},{3,2},{4,5},{5,4},{6,7},{7,6},{8,9},{9,8},{10,11... | collective-permute-start | bytes 196616 | tf_op jit(solution)/shard_map/ppermute | solution.py:288
  9.6 4.0 %collective-permute-start.2 = (bf16[128,256]{1,0:T(8,128)(2,1)}, bf16[128,256]{1,0:T(8,128)(2,1)S(1)}, u32[]{:S(2)}, u32[]{:S(2)}) collective-permute-start(bf16[128,256]{1,0:T(8,128)(2,1)} %param.9), channel_id=1, source_target_pairs={{0,1},{1,0},{2,3},{3,2},{4,5},{5,4},{6,7},{7,6},{8,9},{9,8},{10,11... | collective-permute-start | bytes 196616 | tf_op jit(solution)/shard_map/ppermute | solution.py:288
  12.6 1.0 %copy-start = (bf16[128,1536]{1,0:T(8,128)(2,1)S(1)}, bf16[128,1536]{1,0:T(8,128)(2,1)}, u32[]{:S(2)}) copy-start(bf16[128,1536]{1,0:T(8,128)(2,1)} %q_ref.1) | copy-start | bytes 1179652
  13.8 6.8 %collective-permute-start.4 = (bf16[288,256]{1,0:T(8,128)(2,1)S(1)}, bf16[288,256]{1,0:T(8,128)(2,1)S(1)}, u32[]{:S(2)}, u32[]{:S(2)}) collective-permute-start(bf16[288,256]{1,0:T(8,128)(2,1)S(1)} %get-tuple-element.54), channel_id=1, source_target_pairs={{0,64},{64,128},{128,192},{192,0},{1,65},{65,129},{129,193},{193,1... | collective-permute-start | bytes 442376 | tf_op jit(solution)/shard_map/ppermute | solution.py:288
  15.1 9.6 %collective-permute-start.5 = (bf16[288,256]{1,0:T(8,128)(2,1)S(1)}, bf16[288,256]{1,0:T(8,128)(2,1)S(1)}, u32[]{:S(2)}, u32[]{:S(2)}) collective-permute-start(bf16[288,256]{1,0:T(8,128)(2,1)S(1)} %get-tuple-element.55), channel_id=1, source_target_pairs={{0,128},{64,192},{128,0},{192,64},{1,129},{65,193},{129,1},{193,65... | collective-permute-start | bytes 442376 | tf_op jit(solution)/shard_map/ppermute | solution.py:288
  17.5 7.2 %collective-permute-start.6 = (bf16[288,256]{1,0:T(8,128)(2,1)S(1)}, bf16[288,256]{1,0:T(8,128)(2,1)S(1)}, u32[]{:S(2)}, u32[]{:S(2)}) collective-permute-start(bf16[288,256]{1,0:T(8,128)(2,1)S(1)} %get-tuple-element.56), channel_id=1, source_target_pairs={{0,192},{64,0},{128,64},{192,128},{1,193},{65,1},{129,65},{193,129... | collective-permute-start | bytes 442376 | tf_op jit(solution)/shard_map/ppermute | solution.py:288
  24.7 8.5 %collective-permute-start.7 = (bf16[4,192,256]{2,1,0:T(8,128)(2,1)S(1)}, bf16[4,192,256]{2,1,0:T(8,128)(2,1)S(1)}, u32[]{:S(2)}, u32[]{:S(2)}) collective-permute-start(bf16[4,192,256]{2,1,0:T(8,128)(2,1)S(1)} %get-tuple-element.57.refs_2_), channel_id=1, source_target_pairs={{0,1},{1,0},{2,3},{3,2},{4,5},{5,4},{6,7},{7,6},{8,9},{9,8},{10,11... | collective-permute-start | bytes 1179656 | tf_op jit(solution)/shard_map/ppermute | solution.py:288
  25.7 6.0 %collective-permute-start.9 = (bf16[4,96,256]{2,1,0:T(8,128)(2,1)S(1)}, bf16[4,96,256]{2,1,0:T(8,128)(2,1)S(1)}, u32[]{:S(2)}, u32[]{:S(2)}) collective-permute-start(bf16[4,96,256]{2,1,0:T(8,128)(2,1)S(1)} %get-tuple-element.58), channel_id=1, source_target_pairs={{0,32},{1,5},{4,36},{5,9},{8,40},{9,13},{12,44},{13,1},{16,0},{17,... | collective-permute-start | bytes 589832 | tf_op jit(solution)/shard_map/ppermute | solution.py:314
  27.1 9.9 %collective-permute-start.8 = (bf16[4,96,256]{2,1,0:T(8,128)(2,1)S(1)}, bf16[4,96,256]{2,1,0:T(8,128)(2,1)S(1)}, u32[]{:S(2)}, u32[]{:S(2)}) collective-permute-start(bf16[4,96,256]{2,1,0:T(8,128)(2,1)S(1)} %get-tuple-element.58), channel_id=1, source_target_pairs={{0,16},{1,13},{4,20},{5,1},{8,24},{9,5},{12,28},{13,9},{16,48},{17... | collective-permute-start | bytes 589832 | tf_op jit(solution)/shard_map/ppermute | solution.py:314
  31.7 5.7 %collective-permute-start.10 = (bf16[4,96,256]{2,1,0:T(8,128)(2,1)S(1)}, bf16[4,96,256]{2,1,0:T(8,128)(2,1)S(1)}, u32[]{:S(2)}, u32[]{:S(2)}) collective-permute-start(bf16[4,96,256]{2,1,0:T(8,128)(2,1)S(1)} %collective-permute-done.9), channel_id=1, source_target_pairs={{0,32},{1,5},{4,36},{5,9},{8,40},{9,13},{12,44},{13,1},{16,0},{17,... | collective-permute-start | bytes 589832 | tf_op jit(solution)/shard_map/ppermute | solution.py:314
  31.9 9.0 %collective-permute-start.12 = (bf16[2,4,96,256]{3,2,1,0:T(8,128)(2,1)S(1)}, bf16[2,4,96,256]{3,2,1,0:T(8,128)(2,1)S(1)}, u32[]{:S(2)}, u32[]{:S(2)}) collective-permute-start(bf16[2,4,96,256]{3,2,1,0:T(8,128)(2,1)S(1)} %pad_maximum_fusion.refs_4_), channel_id=1, source_target_pairs={{0,4},{1,33},{4,8},{5,37},{8,12},{9,41},{12,0},{13,45},{16,20},{17... | collective-permute-start | bytes 1179656 | tf_op jit(solution)/shard_map/ppermute | solution.py:314
  37.5 11.7 %collective-permute-start.11 = (bf16[2,4,96,256]{3,2,1,0:T(8,128)(2,1)S(1)}, bf16[2,4,96,256]{3,2,1,0:T(8,128)(2,1)S(1)}, u32[]{:S(2)}, u32[]{:S(2)}) collective-permute-start(bf16[2,4,96,256]{3,2,1,0:T(8,128)(2,1)S(1)} %pad_maximum_fusion.1.refs_6_), channel_id=1, source_target_pairs={{0,4},{1,33},{4,8},{5,37},{8,12},{9,41},{12,0},{13,45},{16,20},{17... | collective-permute-start | bytes 1179656 | tf_op jit(solution)/shard_map/ppermute | solution.py:314
  41.0 8.4 %collective-permute-start.14 = (bf16[2,4,96,256]{3,2,1,0:T(8,128)(2,1)S(1)}, bf16[2,4,96,256]{3,2,1,0:T(8,128)(2,1)S(1)}, u32[]{:S(2)}, u32[]{:S(2)}) collective-permute-start(bf16[2,4,96,256]{3,2,1,0:T(8,128)(2,1)S(1)} %collective-permute-done.12.refs_7_), channel_id=1, source_target_pairs={{0,4},{1,33},{4,8},{5,37},{8,12},{9,41},{12,0},{13,45},{16,20},{17... | collective-permute-start | bytes 1179656 | tf_op jit(solution)/shard_map/ppermute | solution.py:314
  49.2 8.6 %collective-permute-start.13 = (bf16[2,4,96,256]{3,2,1,0:T(8,128)(2,1)S(1)}, bf16[2,4,96,256]{3,2,1,0:T(8,128)(2,1)S(1)}, u32[]{:S(2)}, u32[]{:S(2)}) collective-permute-start(bf16[2,4,96,256]{3,2,1,0:T(8,128)(2,1)S(1)} %collective-permute-done.11.refs_6_), channel_id=1, source_target_pairs={{0,4},{1,33},{4,8},{5,37},{8,12},{9,41},{12,0},{13,45},{16,20},{17... | collective-permute-start | bytes 1179656 | tf_op jit(solution)/shard_map/ppermute | solution.py:314
  49.4 11.1 %collective-permute-start.15 = (bf16[2,4,96,256]{3,2,1,0:T(8,128)(2,1)S(1)}, bf16[2,4,96,256]{3,2,1,0:T(8,128)(2,1)S(1)}, u32[]{:S(2)}, u32[]{:S(2)}) collective-permute-start(bf16[2,4,96,256]{3,2,1,0:T(8,128)(2,1)S(1)} %collective-permute-done.14.refs_7_), channel_id=1, source_target_pairs={{0,4},{1,33},{4,8},{5,37},{8,12},{9,41},{12,0},{13,45},{16,20},{17... | collective-permute-start | bytes 1179656 | tf_op jit(solution)/shard_map/ppermute | solution.py:314
  57.9 8.6 %collective-permute-start.16 = (bf16[2,4,96,256]{3,2,1,0:T(8,128)(2,1)S(1)}, bf16[2,4,96,256]{3,2,1,0:T(8,128)(2,1)S(1)}, u32[]{:S(2)}, u32[]{:S(2)}) collective-permute-start(bf16[2,4,96,256]{3,2,1,0:T(8,128)(2,1)S(1)} %collective-permute-done.13.refs_6_), channel_id=1, source_target_pairs={{0,4},{1,33},{4,8},{5,37},{8,12},{9,41},{12,0},{13,45},{16,20},{17... | collective-permute-start | bytes 1179656 | tf_op jit(solution)/shard_map/ppermute | solution.py:314
  69.2 5.2 %collective-permute-start.17 = (bf16[4,64,896]{2,1,0:T(8,128)(2,1)S(1)}, bf16[4,64,896]{2,1,0:T(8,128)(2,1)S(1)}, u32[]{:S(2)}, u32[]{:S(2)}) collective-permute-start(bf16[4,64,896]{2,1,0:T(8,128)(2,1)S(1)} %attend.10), channel_id=1, source_target_pairs={{0,1},{1,0},{2,3},{3,2},{4,5},{5,4},{6,7},{7,6},{8,9},{9,8},{10,11... | collective-permute-start | bytes 1376264 | tf_op jit(solution)/shard_map/ppermute | solution.py:288
  74.9 8.4 %collective-permute-start.18 = (bf16[64,768]{1,0:T(8,128)(2,1)S(1)}, bf16[64,768]{1,0:T(8,128)(2,1)S(1)}, u32[]{:S(2)}, u32[]{:S(2)}) collective-permute-start(bf16[64,768]{1,0:T(8,128)(2,1)S(1)} %get-tuple-element.89), channel_id=1, source_target_pairs={{0,0},{128,1},{1,64},{129,65},{64,128},{192,129},{65,192},{193,193... | collective-permute-start | bytes 294920 | tf_op jit(solution)/shard_map/ppermute | solution.py:390
  77.8 5.8 %collective-permute-start.19 = (bf16[64,768]{1,0:T(8,128)(2,1)S(1)}, bf16[64,768]{1,0:T(8,128)(2,1)S(1)}, u32[]{:S(2)}, u32[]{:S(2)}) collective-permute-start(bf16[64,768]{1,0:T(8,128)(2,1)S(1)} %get-tuple-element.90), channel_id=1, source_target_pairs={{1,0},{129,1},{0,64},{128,65},{65,128},{193,129},{64,192},{192,193... | collective-permute-start | bytes 294920 | tf_op jit(solution)/shard_map/ppermute | solution.py:390
  77.8 6.6 %collective-permute-start.20 = (bf16[64,768]{1,0:T(8,128)(2,1)S(1)}, bf16[64,768]{1,0:T(8,128)(2,1)S(1)}, u32[]{:S(2)}, u32[]{:S(2)}) collective-permute-start(bf16[64,768]{1,0:T(8,128)(2,1)S(1)} %get-tuple-element.91), channel_id=1, source_target_pairs={{64,0},{192,1},{65,64},{193,65},{0,128},{128,129},{1,192},{129,193... | collective-permute-start | bytes 294920 | tf_op jit(solution)/shard_map/ppermute | solution.py:390
  80.0 6.6 %collective-permute-start.21 = (bf16[64,768]{1,0:T(8,128)(2,1)S(1)}, bf16[64,768]{1,0:T(8,128)(2,1)S(1)}, u32[]{:S(2)}, u32[]{:S(2)}) collective-permute-start(bf16[64,768]{1,0:T(8,128)(2,1)S(1)} %get-tuple-element.92), channel_id=1, source_target_pairs={{65,0},{193,1},{64,64},{192,65},{1,128},{129,129},{0,192},{128,193... | collective-permute-start | bytes 294920 | tf_op jit(solution)/shard_map/ppermute | solution.py:390
